TPU v7x, 32 devices: a whole 2x2x4 slice. The times are simulated.
32 devices in a mesh: tm: 8 (over z, x), feat: 4 (over y, core).
Axes of the slice: x: 2, y: 2, z: 4, core: 2. Of those that a mesh axis runs over, the one named last changes fastest.
Arguments:
- features: bfloat16 [16384, 512], P('tm'), may hold values from -64 to 64
- seg_lengths: int32 [16], replicated, may hold values from 1 to 4096, 16384 in all
Outputs:
- koopman: float32 [512, 512], P('feat')
- lag_error: float32 [128, 16384], P('feat', 'tm')
All inputs are finite; a program needn't handle non-finite values.
Results may differ from a plain program's by a relative error of at most 0.0037.
Values may be sent and summed in bfloat16 or wider, within the bound.
No kernel may reach another device: no remote copies, remote signals or barrier semaphores. Data moves between devices by JAX's collectives and lax.ppermute only.
A program may use at most 64 MiB of HBM per device.

v0:
```python
import jax
import jax.numpy as jnp
from jax import lax
from jax.sharding import PartitionSpec as P

LAG = 64
NC = 128


RIDGE = 0.05
HIGHEST = lax.Precision.HIGHEST
LEAF_WIDTH = 16


def from_behind(shard, axis, by):
    count = lax.axis_size(axis)
    pairs = [(i, i + by) for i in range(count) if 0 <= i + by < count]
    return lax.ppermute(shard, axis, pairs)


def contract(left_rows, right_rows):
    return lax.dot_general(
        left_rows, right_rows, (((0,), (0,)), ((), ())), preferred_element_type=jnp.float32
    )


def leaf_factor(square):
    width = square.shape[0]
    positions = jnp.arange(width, dtype=jnp.int32)
    lower = jnp.zeros_like(square)
    for column_index in range(width):
        column = square[:, column_index] - jnp.dot(lower, lower[column_index], precision=HIGHEST)
        pivot_value = jnp.sqrt(column[column_index])
        new_column = jnp.where(positions >= column_index, column / pivot_value, 0.0)
        lower = lower.at[:, column_index].set(new_column)
    identity = jnp.eye(width, dtype=jnp.float32)
    inverse = jnp.zeros_like(square)
    for row_index in range(width):
        row_vals = lower[row_index]
        new_row = (identity[row_index] - jnp.dot(row_vals, inverse, precision=HIGHEST)) / row_vals[
            row_index
        ]
        inverse = inverse.at[row_index].set(new_row)
    return (lower, inverse)


def factor_pair(square):
    width = square.shape[0]
    if width <= LEAF_WIDTH:
        return leaf_factor(square)
    half = width // 2
    upper_lower, upper_inverse = factor_pair(square[:half, :half])
    panel = jnp.dot(square[half:, :half], upper_inverse.T, precision=HIGHEST)
    trailing = square[half:, half:] - jnp.dot(panel, panel.T, precision=HIGHEST)
    rest_lower, rest_inverse = factor_pair(trailing)
    corner = -jnp.dot(
        jnp.dot(rest_inverse, panel, precision=HIGHEST), upper_inverse, precision=HIGHEST
    )
    zero_block = jnp.zeros((half, width - half), jnp.float32)
    lower = jnp.concatenate(
        [
            jnp.concatenate([upper_lower, zero_block], axis=1),
            jnp.concatenate([panel, rest_lower], axis=1),
        ],
        axis=0,
    )
    inverse = jnp.concatenate(
        [
            jnp.concatenate([upper_inverse, zero_block], axis=1),
            jnp.concatenate([corner, rest_inverse], axis=1),
        ],
        axis=0,
    )
    return (lower, inverse)


def inverse_factor(matrix):
    return factor_pair(matrix)[1]


def shards(features, seg_lengths):
    frame_rows = features.shape[0]
    feat_width = features.shape[1]
    feat_count = lax.axis_size("feat")
    tm_index = lax.axis_index("tm")
    feat_index = lax.axis_index("feat")
    col_block = feat_width // feat_count
    comp_block = NC // feat_count
    head_part = features[:LAG]
    tail_part = from_behind(head_part, "tm", -1)
    ahead_rows = jnp.concatenate([features[LAG:], tail_part], axis=0)
    seg_ends = jnp.cumsum(seg_lengths).astype(jnp.int32)
    moments = tm_index * frame_rows + jnp.arange(frame_rows, dtype=jnp.int32)
    inside = (seg_ends[:, None] > moments[None, :]) & (seg_ends[:, None] <= moments[None, :] + LAG)
    crossing = jnp.sum(inside.astype(jnp.int32), axis=0)
    validity = (crossing == 0).astype(jnp.float32)
    valid_mask = validity.astype(jnp.bfloat16)
    pair_count = jnp.sum(jnp.maximum(seg_lengths - LAG, 0)).astype(jnp.float32)
    local_sums = jnp.stack(
        [
            jnp.dot(valid_mask, features, preferred_element_type=jnp.float32),
            jnp.dot(valid_mask, ahead_rows, preferred_element_type=jnp.float32),
        ]
    )
    total_sums = lax.psum(local_sums, "tm")
    start_col = feat_index * col_block
    lead_mask = lax.dynamic_slice_in_dim(features, start_col, col_block, 1) * valid_mask[:, None]
    ahead_mask = lax.dynamic_slice_in_dim(ahead_rows, start_col, col_block, 1) * valid_mask[:, None]
    gram_a = contract(features, lead_mask) + contract(ahead_rows, ahead_mask)
    gram_b = contract(features, ahead_mask) + contract(ahead_rows, lead_mask)
    summed_a, summed_b = lax.psum((gram_a, gram_b), "tm")
    full_a, full_b = (
        lax.all_gather(summed_a, "feat", axis=1, tiled=True),
        lax.all_gather(summed_b, "feat", axis=1, tiled=True),
    )
    mean_vec = (total_sums[0] + total_sums[1]) / (2.0 * pair_count)
    outer_mean = jnp.outer(mean_vec, mean_vec)
    inst_cov = full_a / (2.0 * pair_count) - outer_mean
    shifted = inst_cov + RIDGE * (jnp.trace(inst_cov) / feat_width) * jnp.eye(
        feat_width, dtype=jnp.float32
    )
    lag_cov = full_b / (2.0 * pair_count) - outer_mean
    lower_inverse = inverse_factor(shifted)
    koopman = jnp.dot(
        jnp.dot(lower_inverse, lag_cov, precision=HIGHEST), lower_inverse.T, precision=HIGHEST
    )
    first_map = lower_inverse[:NC, :].T.astype(jnp.bfloat16)
    second_map = jnp.dot(lower_inverse.T, koopman[:, :NC], precision=HIGHEST).astype(jnp.bfloat16)
    offset = jnp.dot(
        mean_vec, first_map.astype(jnp.float32) - second_map.astype(jnp.float32), precision=HIGHEST
    )
    start_comp = feat_index * comp_block
    first_part = lax.dynamic_slice_in_dim(first_map, start_comp, comp_block, 1)
    second_part = lax.dynamic_slice_in_dim(second_map, start_comp, comp_block, 1)
    offset_part = lax.dynamic_slice_in_dim(offset, start_comp, comp_block, 0)
    forward = jnp.einsum("fc,tf->ct", first_part, ahead_rows, preferred_element_type=jnp.float32)
    backward = jnp.einsum("fc,tf->ct", second_part, features, preferred_element_type=jnp.float32)
    lag_error = (forward - backward - offset_part[:, None]) * validity[None, :]
    koopman_rows = lax.dynamic_slice_in_dim(koopman, start_col, col_block, 0)
    return (koopman_rows, lag_error)


def solution(mesh):
    in_specs = (P("tm", None), P())
    out_specs = (P("feat", None), P("feat", "tm"))
    return jax.shard_map(shards, mesh=mesh, in_specs=in_specs, out_specs=out_specs, check_vma=False)
```

profile of v0, /device:TPU:0, one launch (start us, length us, event | category | flops | bytes accessed | tf_op | source)
XLA Modules:
  0.0 1916.8 jit_solution(8010652638386551120)
XLA Ops:
  11.1 2.7 convolution_bitcast_fusion.1
  16.2 1.6 convolution_add_fusion
  17.8 1.7 fusion.2
  19.5 75.3 %all-reduce.98.cloned.1.call-done = (f32[512,128]{0,1:T(8,128)}, f32[512,128]{0,1:T(8,128)}) async-done(((f32[512,128]{0,1:T(8,128)}, f32[512,128]{0,1:T(8,128)}), (f32[512,128]{0,1:T(8,128)}, f32[512,128]{0,1:T(8,128)})) %all-reduce.98.cloned.1.call-update) | async-done | bytes 524304 | tf_op jit(solution)/shard_map/psum | solution.py:111
  107.1 19.6 %psum.22 = f32[2,512]{1,0:T(2,128)S(1)} all-reduce(f32[2,512]{1,0:T(2,128)S(1)} %pad_maximum_fusion.1), channel_id=1, replica_groups=mesh['tm'=8,'feat'=4] {'tm'}, use_global_device_ids=true, to_apply=%region_5.6 | all-reduce | flops 1024 | bytes 8192 | tf_op jit(solution)/shard_map/psum | solution.py:105
  126.8 2.0 select_reduce_fusion
  180.6 1.5 fusion.1016
  182.1 1.5 fusion.1018
  227.6 1.5 fusion.1030
  242.3 1.5 fusion.1050
  351.0 1.5 fusion.1114
  409.9 1.5 fusion.1146
  567.4 1.5 fusion.1242
  626.8 1.5 fusion.1274
  784.4 1.5 fusion.1370
  843.4 1.5 fusion.1402
  1040.1 1.5 fusion.1512
  1046.1 1.5 fusion.1520
  1047.6 1.5 fusion.1522
  1055.1 1.5 fusion.1532
  1099.3 1.5 fusion.1544
  1105.2 1.5 fusion.1552
  1106.8 1.5 fusion.1554
  1114.3 1.5 fusion.1564
  1205.9 1.5 fusion.1608
  1211.8 1.5 fusion.1616
  1213.3 1.5 fusion.1618
  1220.8 1.5 fusion.1628
  1264.2 1.5 fusion.1640
  1270.1 1.5 fusion.1648
  1271.7 1.5 fusion.1650
  1279.2 1.5 fusion.1660
  1418.4 1.5 fusion.1736
  1424.3 1.5 fusion.1744
  1425.9 1.5 fusion.1746
  1433.5 1.5 fusion.1756
  1477.0 1.5 fusion.1768
  1482.9 1.5 fusion.1776
  1484.5 1.5 fusion.1778
  1491.9 1.5 fusion.1788
  1631.4 1.5 fusion.1864
  1637.3 1.5 fusion.1872
  1638.9 1.5 fusion.1874
  1646.3 1.5 fusion.1884
  1693.8 1.5 fusion.1898
  1699.9 1.5 fusion.1906
  1702.8 1.5 fusion.1910
  1854.6 2.0 fusion.1990
  1857.2 2.0 fusion.1992
  1859.8 2.0 fusion.1994
  1862.4 1.9 fusion.1996
  1864.9 2.0 fusion.1998
  1867.5 2.0 fusion.2000
  1870.2 2.0 fusion.2002
  1872.8 2.0 fusion.2004
  1875.4 2.1 fusion.2006
  1878.2 2.0 fusion.2008
  1880.9 2.1 fusion.2010
  1883.7 2.0 fusion.2012
  1886.3 2.1 fusion.2014
  1889.1 2.1 fusion.2016
  1891.8 2.0 fusion.2018
  1899.4 3.3 fusion.2019
  1902.7 2.9 fusion.3540
  (3862 shorter events, 1370.0 us)
Async XLA Ops:
  7.2 6.7 copy-start
  7.2 87.7 %all-reduce.98.cloned.1.call-start = ((), (), s32[]{:S(2)}) async-start(), calls=%async_computation.2 | async-start | bytes 1048576 | tf_op jit(solution)/shard_map/psum | solution.py:111
  8.2 7.1 collective-permute-start
  14.0 3.8 copy-start.1
  15.3 91.4 %copy-start.21 = (bf16[64,512]{1,0:T(8,128)(2,1)}, bf16[64,512]{1,0:T(8,128)(2,1)S(1)}, u32[]{:S(2)}) copy-start(bf16[64,512]{1,0:T(8,128)(2,1)S(1)} %collective-permute-done) | copy-start | bytes 196612
  17.8 77.2 %copy-start.30 = (s32[16]{0:T(128)S(1)}, s32[16]{0:T(128)}, u32[]{:S(2)}) copy-start(s32[16]{0:T(128)} %param.2051) | copy-start | bytes 196
  19.5 107.4 %all-gather.3.cloned.1.call-start = ((), (), s32[]{:S(2)}) async-start(), calls=%async_computation | async-start | bytes 1310720 | tf_op jit(solution)/shard_map/all_gather | solution.py:113
  94.9 1803.9 %all-gather.5.cloned.1.call-start = ((), (), s32[]{:S(2)}) async-start(), calls=%async_computation.1 | async-start | bytes 1310720 | tf_op jit(solution)/shard_map/all_gather | solution.py:114
  96.2 10.5 copy-start.2
  106.3 61.7 %copy-start.26 = (f32[16,16]{1,0:T(8,128)}, f32[16,16]{1,0:T(8,128)S(1)}, u32[]{:S(2)}) copy-start(f32[16,16]{1,0:T(8,128)S(1)} %fusion.2231) | copy-start | bytes 3076
  168.9 117.9 %copy-start.27 = (f32[16,16]{1,0:T(8,128)S(1)}, f32[16,16]{1,0:T(8,128)}, u32[]{:S(2)}) copy-start(f32[16,16]{1,0:T(8,128)} %copy-done.26) | copy-start | bytes 3076
  899.9 100.2 %copy-start.8 = (f32[32,64]{1,0:T(8,128)}, f32[32,64]{1,0:T(8,128)S(1)}, u32[]{:S(2)}) copy-start(f32[32,64]{1,0:T(8,128)S(1)} %concatenate.2366) | copy-start | bytes 24580
  949.3 50.8 %copy-start.12 = (f32[16,32]{1,0:T(8,128)}, f32[16,32]{1,0:T(8,128)S(1)}, u32[]{:S(2)}) copy-start(f32[16,32]{1,0:T(8,128)S(1)} %concatenate.2367) | copy-start | bytes 6148
  998.9 3.7 copy-start.14
  999.2 0.9 copy-start.6
  1000.1 0.6 copy-start.10
  1001.4 2.7 copy-start.4
  1001.8 154.2 %copy-start.28 = (f32[16,16]{1,0:T(8,128)S(1)}, f32[16,16]{1,0:T(8,128)}, u32[]{:S(2)}) copy-start(f32[16,16]{1,0:T(8,128)} %copy-done.26) | copy-start | bytes 3076
  1673.3 179.1 %copy-start.7 = (f32[32,32]{1,0:T(8,128)S(1)}, f32[32,32]{1,0:T(8,128)}, u32[]{:S(2)}) copy-start(f32[32,32]{1,0:T(8,128)} %copy-done.6) | copy-start | bytes 12292
  1673.3 179.1 %copy-start.9 = (f32[32,64]{1,0:T(8,128)S(1)}, f32[32,64]{1,0:T(8,128)}, u32[]{:S(2)}) copy-start(f32[32,64]{1,0:T(8,128)} %copy-done.8) | copy-start | bytes 24580
  1673.3 179.1 %copy-start.11 = (f32[128,128]{1,0:T(8,128)S(1)}, f32[128,128]{1,0:T(8,128)}, u32[]{:S(2)}) copy-start(f32[128,128]{1,0:T(8,128)} %copy-done.10) | copy-start | bytes 196612
  1673.3 179.1 %copy-start.13 = (f32[16,32]{1,0:T(8,128)S(1)}, f32[16,32]{1,0:T(8,128)}, u32[]{:S(2)}) copy-start(f32[16,32]{1,0:T(8,128)} %copy-done.12) | copy-start | bytes 6148
  1673.3 179.1 %copy-start.15 = (f32[16,16]{1,0:T(8,128)S(1)}, f32[16,16]{1,0:T(8,128)}, u32[]{:S(2)}) copy-start(f32[16,16]{1,0:T(8,128)} %copy-done.14) | copy-start | bytes 3076
  1756.0 97.8 %copy-start.29 = (f32[16,16]{1,0:T(8,128)S(1)}, f32[16,16]{1,0:T(8,128)}, u32[]{:S(2)}) copy-start(f32[16,16]{1,0:T(8,128)} %copy-done.26) | copy-start | bytes 3076
  1804.7 92.1 %copy-start.5 = (f32[256,256]{1,0:T(8,128)S(1)}, f32[256,256]{1,0:T(8,128)}, u32[]{:S(2)}) copy-start(f32[256,256]{1,0:T(8,128)} %copy-done.4) | copy-start | bytes 786436
  1895.5 2.7 copy-start.17
  1895.5 3.9 copy-start.19
  1896.8 1.4 copy-start.23
  1896.8 2.5 copy-start.16
  1898.7 0.7 copy-start.31
  1898.7 4.0 copy-start.18
  1898.7 4.0 copy-start.24
  1902.7 2.9 copy-start.20
  1902.7 2.9 copy-start.32
  1906.5 1.9 copy-start.3
  1906.5 1.9 copy-start.22
  1906.5 1.9 copy-start.25
Sparse Core Ops, SparseCore 0:
  19.6 75.1 all-reduce.97
  96.5 15.9 all-gather.2
  126.9 13.9 all-gather.4
where the time goes:
time: 1950 us; the launch traced here: 1920 us
  matrix products  665 us (34%)
  local copies, waits for them, and re-layouts  484 us (25%)
  between operations  346 us (18%)
  other arithmetic  324 us (17%)
  waiting for transfers between devices  76.7 us (4%)
  blocking collectives  19.6 us (1%)
    dot_general x512, matrix products, leaf_factor(): jnp.dot(row_vals, inverse, precision=HIGHEST)  560 us
    another operation x529, other arithmetic  316 us
    slice x480, local copies, waits for them, and re-layouts, leaf_factor(): pivot_value = jnp.sqrt(column[column_index])  291 us
    slice x480, local copies, waits for them, and re-layouts, leaf_factor(): lower[column_index]  88.1 us
    psum x1, waiting for transfers between devices, shards(): summed_a, summed_b = lax.psum((gram_a, gram_b), 'tm')  75.3 us
    dot_general x481, matrix products, leaf_factor(): jnp.dot(lower, lower[column_index], precision=HIGHEST)  62.5 us
    slice x64, local copies, waits for them, and re-layouts, leaf_factor(): row_vals[row_index]  42.9 us
  transfers between devices with their start and end apart: 4, of which 2 were waited for; matrix products, arithmetic and copies ran while one was open for 76% of the time, Pallas kernels for 0%

commit v1 on v0

v1 whole, which is shorter than its diff:
```python
import functools

import jax
import jax.numpy as jnp
from jax import lax
from jax.experimental import pallas as pl
from jax.experimental.pallas import tpu as pltpu
from jax.sharding import PartitionSpec as P

LAG = 64
NC = 128
RIDGE = 0.05
HIGHEST = lax.Precision.HIGHEST
B = 128
PICKS = 3
F32 = jnp.float32
BF16 = jnp.bfloat16
VMEM_LIMIT = 48 * 2**20


def dot_nn(left, right):
    return jnp.dot(left, right, precision=HIGHEST, preferred_element_type=F32)


def dot_nt(left, right):
    return lax.dot_general(
        left, right, (((1,), (1,)), ((), ())), precision=HIGHEST, preferred_element_type=F32
    )


def contract(left_rows, right_rows):
    return lax.dot_general(
        left_rows, right_rows, (((0,), (0,)), ((), ())), preferred_element_type=F32
    )


def valid_at(seg_ref, moments):
    def step(k, carry):
        end, crossing = carry
        end = end + seg_ref[k]
        hit = (end > moments) & (end <= moments + LAG)
        return end, jnp.where(hit, 1.0, crossing)

    zero = jnp.zeros(moments.shape, F32)
    _, crossing = lax.fori_loop(0, seg_ref.shape[0], step, (jnp.int32(0), zero))
    return 1.0 - crossing


def gram_kernel(chunk_rows, seg_ref, x_ref, halo_ref, out_ref, z_ref):
    frames = x_ref.shape[0]
    feat_count = x_ref.shape[1] // B
    groups = frames // B
    first = lax.axis_index("tm") * frames
    feat = lax.axis_index("feat")
    cols = pl.ds(pl.multiple_of(feat * B, B), B)
    moments = (
        first
        + lax.broadcasted_iota(jnp.int32, (groups, B), 0) * B
        + lax.broadcasted_iota(jnp.int32, (groups, B), 1)
    )
    ahead = valid_at(seg_ref, moments)
    behind = jnp.where(moments >= LAG, valid_at(seg_ref, moments - LAG), 0.0)
    local_behind = jnp.where(moments - first >= LAG, behind, 0.0)
    stacked = jnp.concatenate(
        [ahead, local_behind, ahead + behind, jnp.zeros((B - 3 * groups, B), F32)], axis=0
    )
    columns = stacked.T

    def weight(row):
        return jnp.broadcast_to(columns[:, row : row + 1], (B, B))

    total = jnp.zeros((8, B), F32)
    half = B - LAG
    for g in range(groups):
        low = g * B
        own = x_ref[low : low + B, cols].astype(F32)
        if g + 1 < groups:
            later = x_ref[low + LAG : low + LAG + B, cols].astype(F32)
        else:
            later = jnp.concatenate(
                [x_ref[low + LAG : low + B, cols], halo_ref[:, cols]], axis=0
            ).astype(F32)
        if g > 0:
            earlier = x_ref[low - LAG : low - LAG + B, cols].astype(F32)
        else:
            earlier = jnp.concatenate(
                [x_ref[0:LAG, cols], x_ref[0:half, cols]], axis=0
            ).astype(F32)
        weighted = own * weight(2 * groups + g)
        z_ref[low : low + B, 0:B] = weighted.astype(BF16)
        z_ref[low : low + B, B : 2 * B] = (later * weight(g)).astype(BF16)
        z_ref[low : low + B, 2 * B : 3 * B] = (earlier * weight(groups + g)).astype(BF16)
        for part in range(B // 8):
            total = total + weighted[8 * part : 8 * part + 8]
    tail = x_ref[frames - LAG : frames, cols].astype(F32) * weight(groups - 1)[half:]
    tail = tail.astype(BF16)
    rows = []
    for back in range(PICKS):
        block = lax.rem(feat - back + feat_count, feat_count)
        left = pl.ds(pl.multiple_of(block * B, B), B)
        prod = contract(x_ref[:, left], z_ref[...])
        gram_b = prod[:, B : 2 * B] + prod[:, 2 * B :] + contract(halo_ref[:, left], tail)
        out_ref[back * B : (back + 1) * B, :] = prod[:, :B]
        out_ref[(PICKS + back) * B : (PICKS + back + 1) * B, :] = gram_b
    rows = 2 * PICKS * B
    out_ref[rows : rows + 8, :] = jnp.broadcast_to(jnp.sum(total, axis=0, keepdims=True), (8, B))
    if out_ref.shape[0] > rows + 8:
        out_ref[rows + 8 :, :] = jnp.zeros((out_ref.shape[0] - rows - 8, B), F32)


def across(tile, lane):
    return jnp.broadcast_to(tile[:, lane : lane + 1], tile.shape)


def down(tile, row):
    return jnp.broadcast_to(tile[row : row + 1, :], tile.shape)


def leaf_inverse(square):
    count = square.shape[0] // 8
    lanes = lax.broadcasted_iota(jnp.int32, (8, B), 1)
    sublanes = lax.broadcasted_iota(jnp.int32, (8, B), 0)
    rows = [square[8 * i : 8 * i + 8, :] for i in range(count)]
    extra = [jnp.where(lanes == sublanes + 8 * i, 1.0, 0.0).astype(F32) for i in range(count)]
    result = []
    for b in range(count):
        panel = [across(rows[b], 8 * b + j) for j in range(8)]
        diag = [[down(panel[j], i) if j <= i else None for j in range(8)] for i in range(8)]
        top = [down(rows[b], i) for i in range(8)]
        top_extra = [down(extra[b], i) for i in range(8)]
        below = {k: [across(rows[k], 8 * b + j) for j in range(8)] for k in range(b + 1, count)}
        finished = None
        for i in range(8):
            recip = 1.0 / diag[i][i]
            scale = lax.rsqrt(diag[i][i])
            factor = [None] * 8
            for k in range(i + 1, 8):
                factor[k] = diag[k][i] * recip
            for k in range(i + 1, 8):
                for col in range(i + 1, k + 1):
                    diag[k][col] = diag[k][col] - factor[k] * diag[col][i]
                top[k] = top[k] - factor[k] * top[i]
                top_extra[k] = top_extra[k] - factor[k] * top_extra[i]
            scaled = top_extra[i] * scale
            finished = scaled if finished is None else jnp.where(sublanes == i, scaled, finished)
            for k in range(b + 1, count):
                col_vals = below[k]
                gain = col_vals[i] * recip
                rows[k] = rows[k] - gain * top[i]
                extra[k] = extra[k] - gain * top_extra[i]
                for col in range(i + 1, 8):
                    col_vals[col] = col_vals[col] - gain * diag[col][i]
        result.append(finished)
    return jnp.concatenate(result, axis=0)


def solve_kernel(
    tm_count, seg_ref, sums_ref, x_ref, halo_ref, koop_ref, err_ref, flat_ref, w_ref, b_ref
):
    frames, width = x_ref.shape
    n = width // B
    feat_count = n
    chunk = sums_ref.shape[1]
    first = lax.axis_index("tm") * frames
    feat = lax.axis_index("feat")
    for j in range(tm_count):
        for f in range(feat_count):
            flat_ref[f, j * chunk : (j + 1) * chunk, :] = sums_ref[j * feat_count + f]

    def add_pairs(k, total):
        return total + jnp.maximum(seg_ref[k] - LAG, 0)

    pairs = lax.fori_loop(0, seg_ref.shape[0], add_pairs, jnp.int32(0))
    ones = jnp.ones((8, B), F32)
    inv_pairs = (1.0 / (ones * (2.0 * pairs.astype(F32))))[0:1, :]
    mean_row = [flat_ref[f, 2 * PICKS * B : 2 * PICKS * B + 1, :] * inv_pairs for f in range(n)]
    mean_col = [jnp.broadcast_to(mean_row[f], (B, B)).T for f in range(n)]

    def moment(base, i, j):
        back = (j - i) % n
        if back < PICKS:
            block = flat_ref[j, (base + back) * B : (base + back + 1) * B, :]
        else:
            block = flat_ref[i, (base + n - back) * B : (base + n - back + 1) * B, :].T
        return block * inv_pairs - mean_col[i] * mean_row[j]

    eye = (
        lax.broadcasted_iota(jnp.int32, (B, B), 0) == lax.broadcasted_iota(jnp.int32, (B, B), 1)
    )
    upper = {(i, j): moment(0, i, j) for i in range(n) for j in range(i, n)}
    diag_sum = sum(jnp.where(eye, upper[i, i], 0.0) for i in range(n))
    trace = jnp.sum(jnp.sum(diag_sum, axis=0, keepdims=True), axis=1, keepdims=True)
    ridge = jnp.where(eye, jnp.broadcast_to(RIDGE * (trace / width), (B, B)), 0.0)
    for i in range(n):
        upper[i, i] = upper[i, i] + ridge
    for i in range(n):
        for j in range(n):
            b_ref[i * B : (i + 1) * B, j * B : (j + 1) * B] = moment(PICKS, i, j)

    extra = {}
    for k in range(n):
        inv = leaf_inverse(upper[k, k])
        w_rows = {j: dot_nn(inv, extra[k, j]) for j in range(k)}
        w_rows[k] = inv
        for j in range(n):
            piece = w_rows[j] if j <= k else jnp.zeros((B, B), F32)
            w_ref[k * B : (k + 1) * B, j * B : (j + 1) * B] = piece
        right = {i: dot_nn(inv, upper[k, i]) for i in range(k + 1, n)}
        for i in range(k + 1, n):
            left = right[i].T
            for j in range(i, n):
                upper[i, j] = upper[i, j] - dot_nn(left, right[j])
            for j in range(k + 1):
                update = dot_nn(left, w_rows[j])
                extra[i, j] = extra[i, j] - update if j < k else -update

    comp_block = NC // feat_count
    feat_rows = pl.ds(pl.multiple_of(feat * B, B), B)
    comp_rows = pl.ds(pl.multiple_of(feat * comp_block, comp_block), comp_block)
    lead = jnp.concatenate([w_ref[feat_rows, :], w_ref[comp_rows, :]], axis=0)
    lagged = dot_nn(lead, b_ref[...])
    koop = dot_nt(lagged, w_ref[...])
    koop_ref[...] = koop[:B]
    first_map = w_ref[comp_rows, :].astype(BF16)
    second_map = dot_nn(koop[B:], w_ref[...]).astype(BF16)
    mean_all = jnp.concatenate(mean_row, axis=1)
    offset = jnp.sum(
        mean_all * (first_map.astype(F32) - second_map.astype(F32)), axis=1, keepdims=True
    )

    def apply(maps, frames_block):
        return lax.dot_general(
            maps, frames_block, (((1,), (1,)), ((), ())), preferred_element_type=F32
        )

    step = 256
    for low in range(0, frames, step):
        moments = first + low + lax.broadcasted_iota(jnp.int32, (1, step), 1)
        validity = valid_at(seg_ref, moments)
        backward = apply(second_map, x_ref[low : low + step, :])
        if low + step < frames:
            ahead = x_ref[low + LAG : low + LAG + step, :]
        else:
            ahead = jnp.concatenate([x_ref[low + LAG : frames, :], halo_ref[...]], axis=0)
        forward = apply(first_map, ahead)
        err_ref[:, low : low + step] = (forward - backward - offset) * validity


def shards(features, seg_lengths):
    frames, width = features.shape
    tm_count = lax.axis_size("tm")
    feat_count = lax.axis_size("feat")
    halo = lax.ppermute(features[:LAG], "tm", [(i, i - 1) for i in range(1, tm_count)])
    needed = 2 * PICKS * B + 8
    chunk = -(-needed // (8 * tm_count)) * 8
    vmem = pl.BlockSpec(memory_space=pltpu.VMEM)
    smem = pl.BlockSpec(memory_space=pltpu.SMEM)
    params = pltpu.CompilerParams(vmem_limit_bytes=VMEM_LIMIT)
    partial = pl.pallas_call(
        functools.partial(gram_kernel, chunk),
        out_shape=jax.ShapeDtypeStruct((tm_count * chunk, B), F32),
        in_specs=[smem, vmem, vmem],
        out_specs=vmem,
        scratch_shapes=[pltpu.VMEM((frames, 3 * B), BF16)],
        compiler_params=params,
        name="grams",
    )(seg_lengths, features, halo)
    swapped = lax.all_to_all(partial.reshape(tm_count, chunk, B), "tm", 0, 0)
    summed = jnp.sum(swapped, axis=0)
    spread = jnp.broadcast_to(summed[None], (tm_count * feat_count, chunk, B))
    sums = lax.all_to_all(spread, ("tm", "feat"), 0, 0)
    return pl.pallas_call(
        functools.partial(solve_kernel, tm_count),
        out_shape=[
            jax.ShapeDtypeStruct((width // feat_count, width), F32),
            jax.ShapeDtypeStruct((NC // feat_count, frames), F32),
        ],
        in_specs=[smem, vmem, vmem, vmem],
        out_specs=[vmem, vmem],
        scratch_shapes=[
            pltpu.VMEM((feat_count, tm_count * chunk, B), F32),
            pltpu.VMEM((width, width), F32),
            pltpu.VMEM((width, width), F32),
        ],
        compiler_params=params,
        name="solve",
    )(seg_lengths, sums, features, halo)


def solution(mesh):
    in_specs = (P("tm", None), P())
    out_specs = (P("feat", None), P("feat", "tm"))
    return jax.shard_map(shards, mesh=mesh, in_specs=in_specs, out_specs=out_specs, check_vma=False)
```

time: 1950 us -> 104 us (0.05); the launches traced: 1920 us -> 103 us
  matrix products: 665 us -> 0 us
  local copies, waits for them, and re-layouts: 484 us -> 3.22 us
  between operations: 346 us -> 0.68 us
  other arithmetic: 324 us -> 0.03 us
  waiting for transfers between devices: 76.7 us -> 5.78 us
  blocking collectives: 19.6 us -> 61.1 us
  Pallas kernels: 0 us -> 31.2 us
    dot_general x1129 -> x0, matrix products: 665 us -> none  [the longest x512 560 us: leaf_factor(): jnp.dot(row_vals, inverse, precision=HIGHEST)]
    slice x1058 -> x1, local copies, waits for them, and re-layouts: 438 us -> 0.85 us  [shards(): features[:LAG]]
    another operation x530 -> x0, other arithmetic: 316 us -> none
    psum x1 -> x0, waiting for transfers between devices: 75.3 us -> none  [shards(): summed_a, summed_b = lax.psum((gram_a, gram_b), 'tm')]
    all_to_all x0 -> x2, blocking collectives: none -> 61.1 us  [the longest x1 43.6 us: shards(): sums = lax.all_to_all(spread, ('tm', 'feat'), 0, 0)]
    scatter x1024 -> x0, local copies, waits for them, and re-layouts: 41.9 us -> none  [the longest x512 22.5 us: leaf_factor(): inverse = inverse.at[row_index].set(new_row)]
    pallas_call x0 -> x2, Pallas kernels: none -> 31.2 us  [the longest x1 28.1 us: shards(): pl.pallas_call(functools.partial(solve_kernel, tm_count), out_shape=[jax....]
    psum x1 -> x0, blocking collectives: 19.6 us -> none  [shards(): total_sums = lax.psum(local_sums, 'tm')]
  transfers between devices with their start and end apart: 4 -> 1, of which waited for: 2 -> 1; matrix products, arithmetic and copies ran while one was open for 76% -> 0% of each run, Pallas kernels for 0% -> 0%
where the time goes in v1:
time: 104 us; the launch traced here: 103 us
  blocking collectives  61.1 us (59%)
  Pallas kernels  31.2 us (30%)
  waiting for transfers between devices  5.78 us (6%)
  local copies, waits for them, and re-layouts  3.22 us (3%)
  starting transfers between devices  1.28 us (1%)
    all_to_all x1, blocking collectives, shards(): sums = lax.all_to_all(spread, ('tm', 'feat'), 0, 0)  43.6 us
    pallas_call x1, Pallas kernels, shards(): pl.pallas_call(functools.partial(solve_kernel, tm_count), out_shape=[jax....  28.1 us
    all_to_all x1, blocking collectives, shards(): swapped = lax.all_to_all(partial.reshape(tm_count, chunk, B), 'tm', 0, 0)  17.5 us
    ppermute x1, waiting for transfers between devices, shards(): lax.ppermute(features[:LAG], 'tm', [(i, i - 1) for i in range(1, tm_count)])  5.78 us
    pallas_call x1, Pallas kernels, shards(): pl.pallas_call(functools.partial(gram_kernel, chunk), out_shape=jax.Shape...  3.02 us
    unnamed x8, local copies, waits for them, and re-layouts  2.26 us
  transfers between devices with their start and end apart: 1, of which 1 were waited for; matrix products, arithmetic and copies ran while one was open for 0% of the time, Pallas kernels for 0%

profile of v1, /device:TPU:0, one launch (start us, length us, event | category | flops | bytes accessed | tf_op | source)
XLA Modules:
  0.0 103.2 jit_solution(1844081176295064266)
XLA Ops:
  0.6 0.8 slice.3
  1.5 1.3 %collective-permute-start = (bf16[64,512]{1,0:T(8,128)(2,1)S(1)}, bf16[64,512]{1,0:T(8,128)(2,1)S(1)}, u32[]{:S(2)}, u32[]{:S(2)}) collective-permute-start(bf16[64,512]{1,0:T(8,128)(2,1)S(1)} %slice.3), channel_id=1, source_target_pairs={{4,0},{8,4},{12,8},{16,12},{20,16},{24,20},{28,24},{5,1},{9,5},{13... | collective-permute-start | bytes 196616 | tf_op jit(solution)/shard_map/ppermute | solution.py:253
  2.8 5.8 %collective-permute-done.halo_ref = bf16[64,512]{1,0:T(8,128)(2,1)S(1)} collective-permute-done((bf16[64,512]{1,0:T(8,128)(2,1)S(1)}, bf16[64,512]{1,0:T(8,128)(2,1)S(1)}, u32[]{:S(2)}, u32[]{:S(2)}) %collective-permute-start) | collective-permute-done | bytes 65568 | tf_op jit(solution)/shard_map/ppermute | solution.py:253
  8.5 0.0 copy-start
  8.6 1.6 %copy-done = bf16[2048,512]{1,0:T(8,128)(2,1)S(1)} copy-done((bf16[2048,512]{1,0:T(8,128)(2,1)S(1)}, bf16[2048,512]{1,0:T(8,128)(2,1)}, u32[]{:S(2)}) %copy-start) | copy-done | bytes 2097176
  10.1 0.0 copy-start.2
  10.1 0.7 copy-done.2
  10.8 3.0 %grams.1 = f32[832,128]{1,0:T(8,128)S(1)} custom-call(s32[16]{0:T(128)S(1)} %copy-done.2, bf16[2048,512]{1,0:T(8,128)(2,1)S(1)} %copy-done, bf16[64,512]{1,0:T(8,128)(2,1)S(1)} %collective-permute-done.halo_ref), custom_call_target="tpu_custom_call" | custom-call | tf_op jit(solution)/shard_map/grams/pallas_call | solution.py:259
  13.8 17.5 %all_to_all.10 = f32[8,104,128]{2,1,0:T(8,128)S(1)} all-to-all(f32[8,104,128]{2,1,0:T(8,128)S(1)} %bitcast.1), channel_id=1, replica_groups=mesh['tm'=8,'feat'=4] {'tm'}, dimensions={0} | all-to-all | bytes 851968 | tf_op jit(solution)/shard_map/all_to_all | solution.py:268
  31.3 0.1 broadcast_in_dim.2
  31.5 0.0 copy-start.1
  31.5 0.0 copy-start.3
  31.5 43.6 %all_to_all.11.sums_ref = f32[32,104,128]{2,1,0:T(8,128)S(1)} all-to-all(f32[32,104,128]{2,1,0:T(8,128)S(1)} %broadcast_in_dim.2), channel_id=1, replica_groups=mesh['tm'=8,'feat'=4] {'tm','feat'}, dimensions={0} | all-to-all | bytes 3407872 | tf_op jit(solution)/shard_map/all_to_all | solution.py:271
  75.1 0.0 copy-done.1
  75.1 0.0 copy-done.3
  75.1 28.1 %solve.1 = (f32[128,512]{1,0:T(8,128)}, f32[32,2048]{1,0:T(8,128)}) custom-call(s32[16]{0:T(128)S(1)} %copy-done.3, f32[32,104,128]{2,1,0:T(8,128)S(1)} %all_to_all.11.sums_ref, bf16[2048,512]{1,0:T(8,128)(2,1)S(1)} %copy-done.1, bf16[64,512]{1,0:T(8,128)(2,1)S(1)} %collective-permute-done.halo_ref), custom_call_target="tpu_custom_call" | custom-call | tf_op jit(solution)/shard_map/solve/pallas_call | solution.py:272
  (1 shorter events, 0.0 us)
Async XLA Ops:
  1.5 7.1 %collective-permute-start = (bf16[64,512]{1,0:T(8,128)(2,1)S(1)}, bf16[64,512]{1,0:T(8,128)(2,1)S(1)}, u32[]{:S(2)}, u32[]{:S(2)}) collective-permute-start(bf16[64,512]{1,0:T(8,128)(2,1)S(1)} %slice.3), channel_id=1, source_target_pairs={{4,0},{8,4},{12,8},{16,12},{20,16},{24,20},{28,24},{5,1},{9,5},{13... | collective-permute-start | bytes 196616 | tf_op jit(solution)/shard_map/ppermute | solution.py:253
  8.5 1.6 %copy-start = (bf16[2048,512]{1,0:T(8,128)(2,1)S(1)}, bf16[2048,512]{1,0:T(8,128)(2,1)}, u32[]{:S(2)}) copy-start(bf16[2048,512]{1,0:T(8,128)(2,1)} %x_ref.3) | copy-start | bytes 6291460
  10.1 0.7 copy-start.2
  31.5 43.6 %copy-start.1 = (bf16[2048,512]{1,0:T(8,128)(2,1)S(1)}, bf16[2048,512]{1,0:T(8,128)(2,1)}, u32[]{:S(2)}) copy-start(bf16[2048,512]{1,0:T(8,128)(2,1)} %x_ref.3) | copy-start | bytes 6291460
  31.5 43.6 %copy-start.3 = (s32[16]{0:T(128)S(1)}, s32[16]{0:T(128)}, u32[]{:S(2)}) copy-start(s32[16]{0:T(128)} %seg_ref.3) | copy-start | bytes 196

commit v2 on v1

v2 whole, which is shorter than its diff:
```python
import jax
import jax.numpy as jnp
from jax import lax
from jax.experimental import pallas as pl
from jax.experimental.pallas import tpu as pltpu
from jax.sharding import PartitionSpec as P

LAG = 64
NC = 128
RIDGE = 0.05
HIGHEST = lax.Precision.HIGHEST
B = 128
PICKED = 2 * B + B // 2
LOADS = 8
AHEAD = 2
F32 = jnp.float32
BF16 = jnp.bfloat16
VMEM_LIMIT = 48 * 2**20


def dot_nn(left, right):
    return jnp.dot(left, right, precision=HIGHEST, preferred_element_type=F32)


def dot_nt(left, right):
    return lax.dot_general(
        left, right, (((1,), (1,)), ((), ())), precision=HIGHEST, preferred_element_type=F32
    )


def contract(left_rows, right_rows):
    return lax.dot_general(
        left_rows, right_rows, (((0,), (0,)), ((), ())), preferred_element_type=F32
    )


def valid_at(seg_ref, moments):
    def step(k, carry):
        end, crossing = carry
        end = end + seg_ref[k]
        hit = (end > moments) & (end <= moments + LAG)
        return end, jnp.where(hit, 1.0, crossing)

    zero = jnp.zeros(moments.shape, F32)
    _, crossing = lax.fori_loop(0, seg_ref.shape[0], step, (jnp.int32(0), zero))
    return 1.0 - crossing


def own_block(back):
    feat_count = lax.axis_size("y") * lax.axis_size("c")
    feat = lax.axis_index("y") * lax.axis_size("c") + lax.axis_index("c")
    block = lax.rem(feat - back + feat_count, feat_count)
    return pl.ds(pl.multiple_of(block * B, B), B)


def half_block(square):
    feat = lax.axis_index("y") * lax.axis_size("c") + lax.axis_index("c")
    return jnp.where(feat < 2, square.T[: B // 2], square[B // 2 :])


def frame_start(frames):
    return (lax.axis_index("z") * lax.axis_size("x") + lax.axis_index("x")) * frames


def gram_kernel(seg_hbm, x_hbm, out_ref, tail_ref, total_ref, seg_ref, x_ref, z_ref, sems):
    frames = x_ref.shape[0]
    groups = frames // B
    per = frames // LOADS
    lengths = pltpu.make_async_copy(seg_hbm, seg_ref, sems.at[LOADS])
    lengths.start()
    copies = []
    for c in range(LOADS):
        part = pl.ds(c * per, per)
        copies.append(pltpu.make_async_copy(x_hbm.at[part], x_ref.at[part], sems.at[c]))
        copies[c].start()
    first = frame_start(frames)
    cols = own_block(0)
    lengths.wait()
    moments = (
        first
        + lax.broadcasted_iota(jnp.int32, (groups, B), 0) * B
        + lax.broadcasted_iota(jnp.int32, (groups, B), 1)
    )
    ahead = valid_at(seg_ref, moments)
    behind = jnp.where(moments >= LAG, valid_at(seg_ref, moments - LAG), 0.0)
    local_behind = jnp.where(moments - first >= LAG, behind, 0.0)
    stacked = jnp.concatenate(
        [ahead, local_behind, ahead + behind, jnp.zeros((B - 3 * groups, B), F32)], axis=0
    )
    columns = stacked.T

    def weight(row):
        return jnp.broadcast_to(columns[:, row : row + 1], (B, B))

    total = jnp.zeros((8, B), F32)
    half = B - LAG
    copies[0].wait()
    for c in range(LOADS):
        if c + 1 < LOADS:
            copies[c + 1].wait()
        for g in range(c * per // B, (c + 1) * per // B):
            low = g * B
            own = x_ref[low : low + B, cols].astype(F32)
            if g + 1 < groups:
                later = x_ref[low + LAG : low + LAG + B, cols].astype(F32)
            else:
                later = jnp.concatenate(
                    [x_ref[low + LAG : low + B, cols].astype(F32), jnp.zeros((LAG, B), F32)], axis=0
                )
            if g > 0:
                earlier = x_ref[low - LAG : low - LAG + B, cols].astype(F32)
            else:
                earlier = jnp.concatenate(
                    [jnp.zeros((LAG, B), F32), x_ref[0:half, cols].astype(F32)], axis=0
                )
            weighted = own * weight(2 * groups + g)
            z_ref[low : low + B, 0:B] = weighted.astype(BF16)
            z_ref[low : low + B, B : 2 * B] = (later * weight(g)).astype(BF16)
            z_ref[low : low + B, 2 * B : 3 * B] = (earlier * weight(groups + g)).astype(BF16)
            for part in range(B // 8):
                total = total + weighted[8 * part : 8 * part + 8]
    last = x_ref[frames - LAG : frames, :].astype(F32)
    tail_weight = jnp.concatenate([weight(groups - 1)[half:]] * (last.shape[1] // B), axis=1)
    tail_ref[...] = (last * tail_weight).astype(BF16)
    total_ref[...] = jnp.broadcast_to(jnp.sum(total, axis=0, keepdims=True), (8, B))
    for back in range(3):
        prod = contract(x_ref[:, own_block(back)], z_ref[...])
        for base, gram in ((0, prod[:, :B]), (PICKED, prod[:, B : 2 * B] + prod[:, 2 * B :])):
            if back < 2:
                out_ref[base + back * B : base + (back + 1) * B, :] = gram
            else:
                out_ref[base + 2 * B : base + PICKED, :] = half_block(gram)
    if out_ref.shape[0] > 2 * PICKED:
        out_ref[2 * PICKED :, :] = jnp.zeros((out_ref.shape[0] - 2 * PICKED, B), F32)


def sum_places():
    row = lax.broadcasted_iota(jnp.int32, (B, B), 0)
    lane = lax.broadcasted_iota(jnp.int32, (B, B), 1)
    return row, lane, ((row == B - 1) & (lane < B - 1)) | ((row == B - 2) & (lane == 0))


def edge_kernel(part_ref, tail_ref, total_ref, halo_ref, out_ref):
    cols = own_block(0)
    extra = [
        contract(tail_ref[:, own_block(back)], halo_ref[:, cols])
        + contract(halo_ref[:, own_block(back)], tail_ref[:, cols])
        for back in range(3)
    ]
    lows = [PICKED, PICKED + B, PICKED + 2 * B]
    out_ref[:PICKED, :] = part_ref[:PICKED, :]
    row, lane, places = sum_places()
    total = jnp.broadcast_to(total_ref[0:1, :], (B, B))
    total = jnp.where(row == B - 1, total, jnp.broadcast_to(total[:, B - 1 :], (B, B)))
    own = part_ref[lows[0] : lows[1], :] + extra[0]
    out_ref[lows[0] : lows[1], :] = jnp.where(places, total, own)
    out_ref[lows[1] : lows[2], :] = part_ref[lows[1] : lows[2], :] + extra[1]
    high = lows[2] + B // 2
    out_ref[lows[2] : high, :] = part_ref[lows[2] : high, :] + half_block(extra[2])
    if out_ref.shape[0] > high:
        out_ref[high:, :] = part_ref[high:, :]


def across(tile, lane):
    return jnp.broadcast_to(tile[:, lane : lane + 1], tile.shape)


def down(tile, row):
    return jnp.broadcast_to(tile[row : row + 1, :], tile.shape)


def leaf_inverse(square):
    count = square.shape[0] // 8
    lanes = lax.broadcasted_iota(jnp.int32, (8, B), 1)
    subs = lax.broadcasted_iota(jnp.int32, (8, B), 0)
    rows = [square[8 * i : 8 * i + 8, :] for i in range(count)]
    result = []
    carried = {}
    for b in range(count):
        block = (lanes >= 8 * b) & (lanes < 8 * b + 8)
        cols = {
            k: carried[k] if k in carried else [across(rows[k], 8 * b + j) for j in range(8)]
            for k in range(b, count)
        }
        direct = range(b + 1, min(count, b + AHEAD + 1))
        coming = {k: [across(rows[k], 8 * b + 8 + j) for j in range(8)] for k in direct}
        rows[b] = jnp.where(block, jnp.where(lanes - 8 * b == subs, 1.0, 0.0), rows[b])
        for k in range(b + 1, count):
            rows[k] = jnp.where(block, 0.0, rows[k])
        panel = cols[b]
        top = rows[b]
        pivots = None
        for i in range(8):
            pivot = down(panel[i], i)
            recip = 1.0 / pivot
            pivots = pivot if pivots is None else jnp.where(subs == i, pivot, pivots)
            factor = jnp.where(subs > i, panel[i] * recip, 0.0)
            line = down(top, i)
            split = [down(panel[i], j) if j > i else None for j in range(8)]
            for j in range(i + 1, 8):
                panel[j] = panel[j] - factor * split[j]
            if i < 7:
                top = top - factor * line
            if direct:
                right = [down(cols[b + 1][i], j) for j in range(8)]
            for k in direct:
                gain = cols[k][i] * recip
                for j in range(8):
                    coming[k][j] = coming[k][j] - gain * right[j]
                for j in range(i + 1, 8):
                    cols[k][j] = cols[k][j] - gain * split[j]
                rows[k] = rows[k] - gain * line
        result.append(jnp.where(lanes < 8 * b + 8, top * lax.rsqrt(pivots), 0.0))
        if b + AHEAD + 1 < count:
            recips = 1.0 / pivots
            solved = top * recips
            for k in range(7, 0, -1):
                back = jnp.where(subs < k, panel[k] * recips, 0.0)
                solved = solved - back * down(solved, k)
            lines = [down(solved, j) for j in range(8)]
            for k in range(b + AHEAD + 1, count):
                p = [cols[k][j] * lines[j] for j in range(8)]
                rows[k] = rows[k] - (((p[0] + p[1]) + (p[2] + p[3])) + ((p[4] + p[5]) + (p[6] + p[7])))
        carried = coming
    return jnp.concatenate(result, axis=0)


def solve_kernel(seg_ref, *refs):
    sums_refs, (x_ref, halo_ref, koop_hbm, err_hbm) = refs[:8], refs[8:12]
    koop_ref, err_ref, flat_ref, w_ref, b_ref, sems = refs[12:]
    frames, width = x_ref.shape
    n = feat_count = width // B
    lines, chunk = sums_refs[0].shape[:2]
    first = frame_start(frames)
    x, y, c = lax.axis_index("x"), lax.axis_index("y"), lax.axis_index("c")
    feat = y * 2 + c
    for at, sums_ref in enumerate(sums_refs):
        flip_c, flip_x, flip_y = at // 4, (at // 2) % 2, at % 2
        source = (y ^ flip_y) * 2 + (c ^ flip_c)
        for line in range(lines):
            low = pl.multiple_of((line * 2 + (x ^ flip_x)) * chunk, 8)
            flat_ref[source, pl.ds(low, chunk), :] = sums_ref[line]

    def add_pairs(k, total):
        return total + jnp.maximum(seg_ref[k] - LAG, 0)

    pairs = lax.fori_loop(0, seg_ref.shape[0], add_pairs, jnp.int32(0))
    ones = jnp.ones((8, B), F32)
    inv_pairs = (1.0 / (ones * (2.0 * pairs.astype(F32))))[0:1, :]
    row, lane, places = sum_places()
    mean_row = []
    for f in range(n):
        packed = flat_ref[f, PICKED : PICKED + B, :]
        sums = jnp.where(
            lane[:1] < B - 1, packed[B - 1 :], jnp.broadcast_to(packed[B - 2 : B - 1, :1], (1, B))
        )
        mean_row.append(sums * inv_pairs)
        flat_ref[f, PICKED : PICKED + B, :] = jnp.where(places, packed.T, packed)
    mean_col = [jnp.broadcast_to(mean_row[f], (B, B)).T for f in range(n)]

    def summed(base, i, j):
        back = (j - i) % n
        if back < 2:
            return flat_ref[j, base + back * B : base + (back + 1) * B, :]
        if i < j and back == 2:
            low = base + 2 * B
            pieces = [flat_ref[f, low : low + B // 2, :] for f in (i, j)]
            return jnp.concatenate(pieces, axis=0)
        return summed(base, j, i).T

    def moment(base, i, j):
        return summed(base, i, j) * inv_pairs - mean_col[i] * mean_row[j]

    eye = row == lane
    upper = {(i, j): moment(0, i, j) for i in range(n) for j in range(i, n)}
    diag_sum = sum(jnp.where(eye, upper[i, i], 0.0) for i in range(n))
    trace = jnp.sum(jnp.sum(diag_sum, axis=0, keepdims=True), axis=1, keepdims=True)
    ridge = jnp.where(eye, jnp.broadcast_to(RIDGE * (trace / width), (B, B)), 0.0)
    for i in range(n):
        upper[i, i] = upper[i, i] + ridge
    for i in range(n):
        for j in range(n):
            b_ref[i * B : (i + 1) * B, j * B : (j + 1) * B] = moment(PICKED, i, j)

    groups = frames // B
    moments = (
        first
        + lax.broadcasted_iota(jnp.int32, (groups, B), 0) * B
        + lax.broadcasted_iota(jnp.int32, (groups, B), 1)
    )
    validity = valid_at(seg_ref, moments)
    comp_block = NC // feat_count
    comp_rows = pl.ds(pl.multiple_of(feat * comp_block, comp_block), comp_block)
    step = 2 * B

    def apply(maps, frames_block):
        return lax.dot_general(
            maps, frames_block, (((1,), (1,)), ((), ())), preferred_element_type=F32
        )

    extra = {}
    for k in range(n):
        inv = leaf_inverse(upper[k, k])
        w_rows = {j: dot_nn(inv, extra[k, j]) for j in range(k)}
        w_rows[k] = inv
        for j in range(n):
            piece = w_rows[j] if j <= k else jnp.zeros((B, B), F32)
            w_ref[k * B : (k + 1) * B, j * B : (j + 1) * B] = piece
        right = {i: dot_nn(inv, upper[k, i]) for i in range(k + 1, n)}
        for i in range(k + 1, n):
            left = right[i].T
            for j in range(i, n):
                upper[i, j] = upper[i, j] - dot_nn(left, right[j])
            for j in range(k + 1):
                update = dot_nn(left, w_rows[j])
                extra[i, j] = extra[i, j] - update if j < k else -update
        if k == 0:
            first_map = w_ref[comp_rows, :].astype(BF16)
            for low in range(0, frames, step):
                if low + step < frames:
                    ahead = x_ref[low + LAG : low + LAG + step, :B]
                else:
                    ahead = jnp.concatenate(
                        [x_ref[low + LAG : frames, :B], halo_ref[:, :B]], axis=0
                    )
                err_ref[:, low : low + step] = apply(first_map[:, :B], ahead)

    feat_rows = pl.ds(pl.multiple_of(feat * B, B), B)
    lead = jnp.concatenate([w_ref[feat_rows, :], w_ref[comp_rows, :]], axis=0)
    lagged = dot_nn(lead, b_ref[...])
    koop = dot_nt(lagged, w_ref[...])
    koop_ref[...] = koop[:B]
    koop_out = pltpu.make_async_copy(koop_ref, koop_hbm, sems.at[0])
    koop_out.start()
    second_map = dot_nn(koop[B:], w_ref[...]).astype(BF16)
    mean_all = jnp.concatenate(mean_row, axis=1)
    offset = jnp.sum(
        mean_all * (first_map.astype(F32) - second_map.astype(F32)), axis=1, keepdims=True
    )

    parts = 2
    copies = []
    for part in range(parts):
        span = slice(part * frames // parts, (part + 1) * frames // parts)
        for low in range(span.start, span.stop, step):
            backward = apply(second_map, x_ref[low : low + step, :])
            residual = err_ref[:, low : low + step] - backward - offset
            for at in range(step // B):
                g = low // B + at
                keep = jnp.broadcast_to(validity[g : g + 1], (comp_block, B))
                err_ref[:, g * B : (g + 1) * B] = residual[:, at * B : (at + 1) * B] * keep
        copies.append(
            pltpu.make_async_copy(err_ref.at[:, span], err_hbm.at[:, span], sems.at[1 + part])
        )
        copies[part].start()
    koop_out.wait()
    for copy in copies:
        copy.wait()


def swap(shard, *axes):
    last = 2 ** len(axes) - 1
    return lax.ppermute(shard, axes, [(i, last - i) for i in range(last + 1)])


def shards(features, seg_lengths):
    frames, width = features.shape
    line_count = lax.axis_size("z")
    tm_count = line_count * lax.axis_size("x")
    feat_count = lax.axis_size("y") * lax.axis_size("c")
    halo = lax.ppermute(features[:LAG], ("z", "x"), [(i, i - 1) for i in range(1, tm_count)])
    chunk = -(-2 * PICKED // (8 * tm_count)) * 8
    vmem = pl.BlockSpec(memory_space=pltpu.VMEM)
    smem = pl.BlockSpec(memory_space=pltpu.SMEM)
    params = pltpu.CompilerParams(vmem_limit_bytes=VMEM_LIMIT)
    anywhere = pl.BlockSpec(memory_space=pl.ANY)
    partial, tail, total = pl.pallas_call(
        gram_kernel,
        out_shape=[
            jax.ShapeDtypeStruct((tm_count * chunk, B), F32),
            jax.ShapeDtypeStruct((LAG, width), BF16),
            jax.ShapeDtypeStruct((8, B), F32),
        ],
        in_specs=[anywhere, anywhere],
        out_specs=[vmem, vmem, vmem],
        scratch_shapes=[
            pltpu.SMEM(seg_lengths.shape, jnp.int32),
            pltpu.VMEM((frames, width), BF16),
            pltpu.VMEM((frames, 3 * B), BF16),
            pltpu.SemaphoreType.DMA((LOADS + 1,)),
        ],
        compiler_params=pltpu.CompilerParams(vmem_limit_bytes=53 * 2**20),
        cost_estimate=pl.CostEstimate(
            flops=2 * frames * 9 * B * B, bytes_accessed=frames * width * 2, transcendentals=0
        ),
        name="grams",
    )(seg_lengths, features)
    partial = pl.pallas_call(
        edge_kernel,
        out_shape=jax.ShapeDtypeStruct((tm_count * chunk, B), F32),
        in_specs=[vmem] * 4,
        out_specs=vmem,
        compiler_params=params,
        name="edges",
    )(partial, tail, total, halo)
    swapped = lax.all_to_all(partial.reshape(tm_count, chunk, B), ("z", "x"), 0, 0)
    summed = jnp.sum(swapped, axis=0)
    spread = jnp.broadcast_to(summed[None], (line_count, chunk, B))
    line = lax.all_to_all(spread, "z", 0, 0)
    held = [line, swap(line, "y"), swap(line, "x"), swap(line, "x", "y")]
    held = held + [swap(part, "c") for part in held]
    return pl.pallas_call(
        solve_kernel,
        out_shape=[
            jax.ShapeDtypeStruct((width // feat_count, width), F32),
            jax.ShapeDtypeStruct((NC // feat_count, frames), F32),
        ],
        in_specs=[smem] + [vmem] * 10,
        out_specs=[anywhere, anywhere],
        scratch_shapes=[
            pltpu.VMEM((width // feat_count, width), F32),
            pltpu.VMEM((NC // feat_count, frames), F32),
            pltpu.VMEM((feat_count, tm_count * chunk, B), F32),
            pltpu.VMEM((width, width), F32),
            pltpu.VMEM((width, width), F32),
            pltpu.SemaphoreType.DMA((3,)),
        ],
        compiler_params=params,
        name="solve",
    )(seg_lengths, *held, features, halo)


def solution(mesh):
    tm, feat = mesh.shape["tm"], mesh.shape["feat"]
    fine = jax.sharding.Mesh(
        mesh.devices.reshape(tm // 2, 2, feat // 2, 2), ("z", "x", "y", "c")
    )
    in_specs = (P(("z", "x"), None), P())
    out_specs = (P(("y", "c"), None), P(("y", "c"), ("z", "x")))
    return jax.shard_map(shards, mesh=fine, in_specs=in_specs, out_specs=out_specs, check_vma=False)
```

time: 104 us -> 64.9 us (0.62)
  blocking collectives: 61.1 us -> 26.6 us
  Pallas kernels: 31.2 us -> 23 us
  starting transfers between devices: 1.28 us -> 5.15 us
  local copies, waits for them, and re-layouts: 3.22 us -> 1.52 us
  waiting for transfers between devices: 5.78 us -> 7.46 us
    all_to_all x2, blocking collectives: 61.1 us -> 26.6 us  [the longest x1 17.4 us: shards(): lax.all_to_all(partial.reshape(tm_count, chunk, B), ('z', 'x'), 0, 0)]
    pallas_call x2 -> x3, Pallas kernels: 31.2 us -> 23 us  [the longest x1 19.1 us: shards(): pl.pallas_call(solve_kernel, out_shape=[jax.ShapeDtypeStruct((width // fe...]
    ppermute x1 -> x8, starting transfers between devices: 1.28 us -> 5.15 us  [the longest x7 3.74 us: swap(): return lax.ppermute(shard, axes, [(i, last - i) for i in range(last + 1)])]
    ppermute x1 -> x8, waiting for transfers between devices: 5.78 us -> 7.46 us  [the longest x7 5.97 us: swap(): return lax.ppermute(shard, axes, [(i, last - i) for i in range(last + 1)])]
    unnamed x8 -> x6, local copies, waits for them, and re-layouts: 2.26 us -> 0.66 us
  transfers between devices with their start and end apart: 1 -> 8, of which waited for: 1 -> 6; matrix products, arithmetic and copies ran while one was open for 0% -> 0% of each run, Pallas kernels for 0% -> 6%
where the time goes in v2:
time: 64.9 us; the launch traced here: 64.6 us
  blocking collectives  26.6 us (41%)
  Pallas kernels  23 us (35%)
  waiting for transfers between devices  7.46 us (11%)
  starting transfers between devices  5.15 us (8%)
  local copies, waits for them, and re-layouts  1.52 us (2%)
  between operations  0.86 us (1%)
    pallas_call x1, Pallas kernels, shards(): pl.pallas_call(solve_kernel, out_shape=[jax.ShapeDtypeStruct((width // fe...  19.1 us
    all_to_all x1, blocking collectives, shards(): lax.all_to_all(partial.reshape(tm_count, chunk, B), ('z', 'x'), 0, 0)  17.4 us
    all_to_all x1, blocking collectives, shards(): line = lax.all_to_all(spread, 'z', 0, 0)  9.19 us
    ppermute x7, waiting for transfers between devices, swap(): return lax.ppermute(shard, axes, [(i, last - i) for i in range(last + 1)])  5.97 us
    ppermute x7, starting transfers between devices, swap(): return lax.ppermute(shard, axes, [(i, last - i) for i in range(last + 1)])  3.74 us
    pallas_call x1, Pallas kernels, shards(): pl.pallas_call(gram_kernel, out_shape=[jax.ShapeDtypeStruct((tm_count * c...  3.62 us
    ppermute x1, waiting for transfers between devices, shards(): lax.ppermute(features[:LAG], ('z', 'x'), [(i, i - 1) for i in range(1, tm...  1.5 us
    ppermute x1, starting transfers between devices, shards(): lax.ppermute(features[:LAG], ('z', 'x'), [(i, i - 1) for i in range(1, tm...  1.41 us
  transfers between devices with their start and end apart: 8, of which 6 were waited for; matrix products, arithmetic and copies ran while one was open for 0% of the time, Pallas kernels for 6%

profile of v2, /device:TPU:0, one launch (start us, length us, event | category | flops | bytes accessed | tf_op | source)
XLA Modules:
  0.0 64.6 jit_solution(14026444536355974130)
XLA Ops:
  0.6 0.8 %slice.3 = bf16[64,512]{1,0:T(8,128)(2,1)S(1)} slice(bf16[2048,512]{1,0:T(8,128)(2,1)} %refs_8_.1), slice={[0:64], [0:512]} | slice | bytes 131072 | tf_op jit(solution)/shard_map/slice | solution.py:371
  1.5 0.0 copy-start
  1.5 1.4 %collective-permute-start = (bf16[64,512]{1,0:T(8,128)(2,1)S(1)}, bf16[64,512]{1,0:T(8,128)(2,1)S(1)}, u32[]{:S(2)}, u32[]{:S(2)}) collective-permute-start(bf16[64,512]{1,0:T(8,128)(2,1)S(1)} %slice.3), channel_id=1, source_target_pairs={{4,0},{8,4},{12,8},{16,12},{20,16},{24,20},{28,24},{5,1},{9,5},{13... | collective-permute-start | bytes 196616 | tf_op jit(solution)/shard_map/ppermute | solution.py:371
  2.9 0.0 copy-start.1
  2.9 0.6 %copy-done.1 = s32[16]{0:T(128)S(1)} copy-done((s32[16]{0:T(128)S(1)}, s32[16]{0:T(128)}, u32[]{:S(2)}) %copy-start.1) | copy-done | bytes 88
  3.6 0.0 copy-start.2
  3.6 3.6 %grams.1 = (f32[640,128]{1,0:T(8,128)S(1)}, bf16[64,512]{1,0:T(8,128)(2,1)S(1)}, f32[8,128]{1,0:T(8,128)S(1)}) custom-call(s32[16]{0:T(128)S(1)} %copy-done.1, bf16[2048,512]{1,0:T(8,128)(2,1)} %refs_8_.1), custom_call_target="tpu_custom_call" | custom-call | flops 603979776 | bytes 2097152 | tf_op jit(solution)/shard_map/grams/pallas_call | solution.py:377
  7.2 1.5 %collective-permute-done.halo_ref.refs_9_ = bf16[64,512]{1,0:T(8,128)(2,1)S(1)} collective-permute-done((bf16[64,512]{1,0:T(8,128)(2,1)S(1)}, bf16[64,512]{1,0:T(8,128)(2,1)S(1)}, u32[]{:S(2)}, u32[]{:S(2)}) %collective-permute-start) | collective-permute-done | bytes 65568 | tf_op jit(solution)/shard_map/ppermute | solution.py:371
  8.7 0.3 edges.1
  9.0 17.4 %all_to_all.10 = f32[8,80,128]{2,1,0:T(8,128)S(1)} all-to-all(f32[8,80,128]{2,1,0:T(8,128)S(1)} %bitcast.1), channel_id=1, replica_groups=mesh['z'=4,'x'=2,'y'=2,'c'=2] {'z','x'}, dimensions={0} | all-to-all | bytes 655360 | tf_op jit(solution)/shard_map/all_to_all | solution.py:406
  26.4 9.2 %all_to_all.11.refs_0_ = f32[4,80,128]{2,1,0:T(8,128)S(1)} all-to-all(f32[4,80,128]{2,1,0:T(8,128)S(1)} %broadcast_in_dim.2), channel_id=1, replica_groups=mesh['z'=4,'x'=2,'y'=2,'c'=2] {'z'}, dimensions={0} | all-to-all | bytes 327680 | tf_op jit(solution)/shard_map/all_to_all | solution.py:409
  35.6 1.8 %collective-permute-start.3 = (f32[4,80,128]{2,1,0:T(8,128)S(1)}, f32[4,80,128]{2,1,0:T(8,128)S(1)}, u32[]{:S(2)}, u32[]{:S(2)}) collective-permute-start(f32[4,80,128]{2,1,0:T(8,128)S(1)} %all_to_all.11.refs_0_), channel_id=1, source_target_pairs={{0,6},{2,4},{4,2},{6,0},{1,7},{3,5},{5,3},{7,1},{8,14},{10,12},{12... | collective-permute-start | bytes 491528 | tf_op jit(solution)/shard_map/ppermute | solution.py:363
  37.4 1.2 %collective-permute-start.2 = (f32[4,80,128]{2,1,0:T(8,128)S(1)}, f32[4,80,128]{2,1,0:T(8,128)S(1)}, u32[]{:S(2)}, u32[]{:S(2)}) collective-permute-start(f32[4,80,128]{2,1,0:T(8,128)S(1)} %all_to_all.11.refs_0_), channel_id=1, source_target_pairs={{0,4},{4,0},{1,5},{5,1},{2,6},{6,2},{3,7},{7,3},{8,12},{12,8},{9,1... | collective-permute-start | bytes 491528 | tf_op jit(solution)/shard_map/ppermute | solution.py:363
  38.6 0.5 collective-permute-start.1
  39.1 0.0 collective-permute-start.4
  39.1 2.7 %collective-permute-done.3.refs_3_ = f32[4,80,128]{2,1,0:T(8,128)S(1)} collective-permute-done((f32[4,80,128]{2,1,0:T(8,128)S(1)}, f32[4,80,128]{2,1,0:T(8,128)S(1)}, u32[]{:S(2)}, u32[]{:S(2)}) %collective-permute-start.3) | collective-permute-done | bytes 163872 | tf_op jit(solution)/shard_map/ppermute | solution.py:363
  41.8 0.0 collective-permute-start.7
  41.8 1.8 %collective-permute-done.2.refs_2_ = f32[4,80,128]{2,1,0:T(8,128)S(1)} collective-permute-done((f32[4,80,128]{2,1,0:T(8,128)S(1)}, f32[4,80,128]{2,1,0:T(8,128)S(1)}, u32[]{:S(2)}, u32[]{:S(2)}) %collective-permute-start.2) | collective-permute-done | bytes 163872 | tf_op jit(solution)/shard_map/ppermute | solution.py:363
  43.7 0.0 collective-permute-start.6
  43.7 0.3 collective-permute-done.1.refs_1_
  43.9 0.2 collective-permute-start.5
  44.2 0.0 collective-permute-done.4.refs_4_
  44.2 0.0 collective-permute-done.7.refs_7_
  44.2 0.9 %collective-permute-done.6.refs_6_ = f32[4,80,128]{2,1,0:T(8,128)S(1)} collective-permute-done((f32[4,80,128]{2,1,0:T(8,128)S(1)}, f32[4,80,128]{2,1,0:T(8,128)S(1)}, u32[]{:S(2)}, u32[]{:S(2)}) %collective-permute-start.6) | collective-permute-done | bytes 163872 | tf_op jit(solution)/shard_map/ppermute | solution.py:363
  45.1 0.3 collective-permute-done.5.refs_5_
  45.3 0.0 copy-done
  45.3 0.0 copy-done.2
  45.3 19.1 %solve.1 = (f32[128,512]{1,0:T(8,128)}, f32[32,2048]{1,0:T(8,128)}) custom-call(s32[16]{0:T(128)S(1)} %copy-done.2, f32[4,80,128]{2,1,0:T(8,128)S(1)} %all_to_all.11.refs_0_, f32[4,80,128]{2,1,0:T(8,128)S(1)} %collective-permute-done.1.refs_1_, f32[4,80,128]{2,1,0:T(8,128)S(1)} %collective-permute-done.2.refs_2_, ...), custom_call_target="tpu_custom_call" | custom-call | tf_op jit(solution)/shard_map/solve/pallas_call | solution.py:412
  (2 shorter events, 0.0 us)
Async XLA Ops:
  1.5 43.9 %copy-start = (bf16[2048,512]{1,0:T(8,128)(2,1)S(1)}, bf16[2048,512]{1,0:T(8,128)(2,1)}, u32[]{:S(2)}) copy-start(bf16[2048,512]{1,0:T(8,128)(2,1)} %refs_8_.1) | copy-start | bytes 6291460
  1.5 7.2 %collective-permute-start = (bf16[64,512]{1,0:T(8,128)(2,1)S(1)}, bf16[64,512]{1,0:T(8,128)(2,1)S(1)}, u32[]{:S(2)}, u32[]{:S(2)}) collective-permute-start(bf16[64,512]{1,0:T(8,128)(2,1)S(1)} %slice.3), channel_id=1, source_target_pairs={{4,0},{8,4},{12,8},{16,12},{20,16},{24,20},{28,24},{5,1},{9,5},{13... | collective-permute-start | bytes 196616 | tf_op jit(solution)/shard_map/ppermute | solution.py:371
  2.9 0.7 %copy-start.1 = (s32[16]{0:T(128)S(1)}, s32[16]{0:T(128)}, u32[]{:S(2)}) copy-start(s32[16]{0:T(128)} %seg_ref.1) | copy-start | bytes 196
  3.6 41.8 %copy-start.2 = (s32[16]{0:T(128)S(1)}, s32[16]{0:T(128)}, u32[]{:S(2)}) copy-start(s32[16]{0:T(128)} %seg_ref.1) | copy-start | bytes 196
  35.6 6.2 %collective-permute-start.3 = (f32[4,80,128]{2,1,0:T(8,128)S(1)}, f32[4,80,128]{2,1,0:T(8,128)S(1)}, u32[]{:S(2)}, u32[]{:S(2)}) collective-permute-start(f32[4,80,128]{2,1,0:T(8,128)S(1)} %all_to_all.11.refs_0_), channel_id=1, source_target_pairs={{0,6},{2,4},{4,2},{6,0},{1,7},{3,5},{5,3},{7,1},{8,14},{10,12},{12... | collective-permute-start | bytes 491528 | tf_op jit(solution)/shard_map/ppermute | solution.py:363
  37.4 6.2 %collective-permute-start.2 = (f32[4,80,128]{2,1,0:T(8,128)S(1)}, f32[4,80,128]{2,1,0:T(8,128)S(1)}, u32[]{:S(2)}, u32[]{:S(2)}) collective-permute-start(f32[4,80,128]{2,1,0:T(8,128)S(1)} %all_to_all.11.refs_0_), channel_id=1, source_target_pairs={{0,4},{4,0},{1,5},{5,1},{2,6},{6,2},{3,7},{7,3},{8,12},{12,8},{9,1... | collective-permute-start | bytes 491528 | tf_op jit(solution)/shard_map/ppermute | solution.py:363
  38.6 5.3 %collective-permute-start.1 = (f32[4,80,128]{2,1,0:T(8,128)S(1)}, f32[4,80,128]{2,1,0:T(8,128)S(1)}, u32[]{:S(2)}, u32[]{:S(2)}) collective-permute-start(f32[4,80,128]{2,1,0:T(8,128)S(1)} %all_to_all.11.refs_0_), channel_id=1, source_target_pairs={{0,2},{2,0},{1,3},{3,1},{4,6},{6,4},{5,7},{7,5},{8,10},{10,8},{9,1... | collective-permute-start | bytes 491528 | tf_op jit(solution)/shard_map/ppermute | solution.py:363
  39.1 5.1 %collective-permute-start.4 = (f32[4,80,128]{2,1,0:T(8,128)S(1)}, f32[4,80,128]{2,1,0:T(8,128)S(1)}, u32[]{:S(2)}, u32[]{:S(2)}) collective-permute-start(f32[4,80,128]{2,1,0:T(8,128)S(1)} %all_to_all.11.refs_0_), channel_id=1, source_target_pairs={{0,1},{1,0},{2,3},{3,2},{4,5},{5,4},{6,7},{7,6},{8,9},{9,8},{10,11... | collective-permute-start | bytes 491528 | tf_op jit(solution)/shard_map/ppermute | solution.py:363
  41.8 2.4 %collective-permute-start.7 = (f32[4,80,128]{2,1,0:T(8,128)S(1)}, f32[4,80,128]{2,1,0:T(8,128)S(1)}, u32[]{:S(2)}, u32[]{:S(2)}) collective-permute-start(f32[4,80,128]{2,1,0:T(8,128)S(1)} %collective-permute-done.3.refs_3_), channel_id=1, source_target_pairs={{0,1},{1,0},{2,3},{3,2},{4,5},{5,4},{6,7},{7,6},{8,9},{9,8},{10,11... | collective-permute-start | bytes 491528 | tf_op jit(solution)/shard_map/ppermute | solution.py:363
  43.7 1.4 %collective-permute-start.6 = (f32[4,80,128]{2,1,0:T(8,128)S(1)}, f32[4,80,128]{2,1,0:T(8,128)S(1)}, u32[]{:S(2)}, u32[]{:S(2)}) collective-permute-start(f32[4,80,128]{2,1,0:T(8,128)S(1)} %collective-permute-done.2.refs_2_), channel_id=1, source_target_pairs={{0,1},{1,0},{2,3},{3,2},{4,5},{5,4},{6,7},{7,6},{8,9},{9,8},{10,11... | collective-permute-start | bytes 491528 | tf_op jit(solution)/shard_map/ppermute | solution.py:363
  43.9 1.4 %collective-permute-start.5 = (f32[4,80,128]{2,1,0:T(8,128)S(1)}, f32[4,80,128]{2,1,0:T(8,128)S(1)}, u32[]{:S(2)}, u32[]{:S(2)}) collective-permute-start(f32[4,80,128]{2,1,0:T(8,128)S(1)} %collective-permute-done.1.refs_1_), channel_id=1, source_target_pairs={{0,1},{1,0},{2,3},{3,2},{4,5},{5,4},{6,7},{7,6},{8,9},{9,8},{10,11... | collective-permute-start | bytes 491528 | tf_op jit(solution)/shard_map/ppermute | solution.py:363

commit v3 on v2

--- a/solution.py
+++ b/solution.py
@@ -11,7 +11,7 @@
 HIGHEST = lax.Precision.HIGHEST
 B = 128
 PICKED = 2 * B + B // 2
-LOADS = 8
+LOADS = 4
 AHEAD = 2
 F32 = jnp.float32
 BF16 = jnp.bfloat16
@@ -20,12 +20,6 @@
 
 def dot_nn(left, right):
     return jnp.dot(left, right, precision=HIGHEST, preferred_element_type=F32)
-
-
-def dot_nt(left, right):
-    return lax.dot_general(
-        left, right, (((1,), (1,)), ((), ())), precision=HIGHEST, preferred_element_type=F32
-    )
 
 
 def contract(left_rows, right_rows):
@@ -42,7 +36,7 @@
         return end, jnp.where(hit, 1.0, crossing)
 
     zero = jnp.zeros(moments.shape, F32)
-    _, crossing = lax.fori_loop(0, seg_ref.shape[0], step, (jnp.int32(0), zero))
+    _, crossing = lax.fori_loop(0, seg_ref.shape[0], step, (jnp.int32(0), zero), unroll=True)
     return 1.0 - crossing
 
 
@@ -227,24 +221,24 @@
 
 def solve_kernel(seg_ref, *refs):
     sums_refs, (x_ref, halo_ref, koop_hbm, err_hbm) = refs[:8], refs[8:12]
-    koop_ref, err_ref, flat_ref, w_ref, b_ref, sems = refs[12:]
+    koop_ref, err_ref, flat_ref, w_ref, wt_ref, t_ref, sems = refs[12:]
     frames, width = x_ref.shape
     n = feat_count = width // B
     lines, chunk = sums_refs[0].shape[:2]
     first = frame_start(frames)
-    x, y, c = lax.axis_index("x"), lax.axis_index("y"), lax.axis_index("c")
+    z, x, y, c = [lax.axis_index(name) for name in ("z", "x", "y", "c")]
     feat = y * 2 + c
     for at, sums_ref in enumerate(sums_refs):
         flip_c, flip_x, flip_y = at // 4, (at // 2) % 2, at % 2
         source = (y ^ flip_y) * 2 + (c ^ flip_c)
         for line in range(lines):
-            low = pl.multiple_of((line * 2 + (x ^ flip_x)) * chunk, 8)
+            low = pl.multiple_of(((z ^ line) * 2 + (x ^ flip_x)) * chunk, 8)
             flat_ref[source, pl.ds(low, chunk), :] = sums_ref[line]
 
     def add_pairs(k, total):
         return total + jnp.maximum(seg_ref[k] - LAG, 0)
 
-    pairs = lax.fori_loop(0, seg_ref.shape[0], add_pairs, jnp.int32(0))
+    pairs = lax.fori_loop(0, seg_ref.shape[0], add_pairs, jnp.int32(0), unroll=True)
     ones = jnp.ones((8, B), F32)
     inv_pairs = (1.0 / (ones * (2.0 * pairs.astype(F32))))[0:1, :]
     row, lane, places = sum_places()
@@ -278,17 +272,6 @@
     ridge = jnp.where(eye, jnp.broadcast_to(RIDGE * (trace / width), (B, B)), 0.0)
     for i in range(n):
         upper[i, i] = upper[i, i] + ridge
-    for i in range(n):
-        for j in range(n):
-            b_ref[i * B : (i + 1) * B, j * B : (j + 1) * B] = moment(PICKED, i, j)
-
-    groups = frames // B
-    moments = (
-        first
-        + lax.broadcasted_iota(jnp.int32, (groups, B), 0) * B
-        + lax.broadcasted_iota(jnp.int32, (groups, B), 1)
-    )
-    validity = valid_at(seg_ref, moments)
     comp_block = NC // feat_count
     comp_rows = pl.ds(pl.multiple_of(feat * comp_block, comp_block), comp_block)
     step = 2 * B
@@ -299,22 +282,49 @@
         )
 
     extra = {}
+    lagged = {}
     for k in range(n):
         inv = leaf_inverse(upper[k, k])
-        w_rows = {j: dot_nn(inv, extra[k, j]) for j in range(k)}
-        w_rows[k] = inv
-        for j in range(n):
-            piece = w_rows[j] if j <= k else jnp.zeros((B, B), F32)
-            w_ref[k * B : (k + 1) * B, j * B : (j + 1) * B] = piece
-        right = {i: dot_nn(inv, upper[k, i]) for i in range(k + 1, n)}
-        for i in range(k + 1, n):
-            left = right[i].T
-            for j in range(i, n):
-                upper[i, j] = upper[i, j] - dot_nn(left, right[j])
-            for j in range(k + 1):
-                update = dot_nn(left, w_rows[j])
-                extra[i, j] = extra[i, j] - update if j < k else -update
         if k == 0:
+            for i in range(n):
+                lagged[i] = jnp.concatenate([moment(PICKED, i, j) for j in range(n)], axis=1)
+        rest = range(k + 1, n)
+        if rest:
+            near = dot_nn(inv, upper[k, k + 1])
+            left = [near.T]
+            upper[k + 1, k + 1] = upper[k + 1, k + 1] - dot_nn(left[0], near)
+        others = [upper[k, i] for i in range(k + 2, n)] + ([extra[k]] if k else []) + [lagged[k]]
+        others = dot_nn(inv, jnp.concatenate(others, axis=1))
+        at = max(n - k - 2, 0) * B
+        far = [others[:, i : i + B] for i in range(0, at, B)]
+        w_rows = jnp.concatenate([others[:, at : at + k * B], inv], axis=1) if k else inv
+        t_rows = others[:, at + k * B :]
+        w_ref[k * B : (k + 1) * B, : (k + 1) * B] = w_rows
+        wt_ref[: (k + 1) * B, k * B : (k + 1) * B] = w_rows.T
+        if k + 1 < n:
+            w_ref[k * B : (k + 1) * B, (k + 1) * B :] = jnp.zeros((B, (n - 1 - k) * B), F32)
+            wt_ref[(k + 1) * B :, k * B : (k + 1) * B] = jnp.zeros(((n - 1 - k) * B, B), F32)
+        t_ref[k * B : (k + 1) * B, :] = t_rows
+        if rest:
+            left = jnp.concatenate(left + [block.T for block in far], axis=0)
+            update = dot_nn(left, jnp.concatenate(far + [w_rows, t_rows], axis=1))
+            for i in rest:
+                line = update[(i - k - 1) * B : (i - k) * B]
+                for j in range(max(i, k + 2), n):
+                    upper[i, j] = upper[i, j] - line[:, (j - k - 2) * B : (j - k - 1) * B]
+                new = -line[:, at + k * B : at + (k + 1) * B]
+                if k:
+                    new = jnp.concatenate([extra[i] - line[:, at : at + k * B], new], axis=1)
+                extra[i] = new
+                lagged[i] = lagged[i] - line[:, at + (k + 1) * B :]
+        if k == 0:
+            groups = frames // B
+            moments = (
+                first
+                + lax.broadcasted_iota(jnp.int32, (groups, B), 0) * B
+                + lax.broadcasted_iota(jnp.int32, (groups, B), 1)
+            )
+            validity = valid_at(seg_ref, moments)
             first_map = w_ref[comp_rows, :].astype(BF16)
             for low in range(0, frames, step):
                 if low + step < frames:
@@ -326,19 +336,22 @@
                 err_ref[:, low : low + step] = apply(first_map[:, :B], ahead)
 
     feat_rows = pl.ds(pl.multiple_of(feat * B, B), B)
-    lead = jnp.concatenate([w_ref[feat_rows, :], w_ref[comp_rows, :]], axis=0)
-    lagged = dot_nn(lead, b_ref[...])
-    koop = dot_nt(lagged, w_ref[...])
+    lead = jnp.concatenate([t_ref[feat_rows, :], t_ref[comp_rows, :]], axis=0)
+    half = width // 2
+    low_cols = dot_nn(lead[:, :half], wt_ref[:half, :half])
+    koop = jnp.concatenate([low_cols, dot_nn(lead, wt_ref[:, half:])], axis=1)
     koop_ref[...] = koop[:B]
     koop_out = pltpu.make_async_copy(koop_ref, koop_hbm, sems.at[0])
     koop_out.start()
-    second_map = dot_nn(koop[B:], w_ref[...]).astype(BF16)
+    low_cols = dot_nn(koop[B:], w_ref[:, :half])
+    high_cols = dot_nn(koop[B:, half:], w_ref[half:, half:])
+    second_map = jnp.concatenate([low_cols, high_cols], axis=1).astype(BF16)
     mean_all = jnp.concatenate(mean_row, axis=1)
     offset = jnp.sum(
         mean_all * (first_map.astype(F32) - second_map.astype(F32)), axis=1, keepdims=True
     )
 
-    parts = 2
+    parts = 4
     copies = []
     for part in range(parts):
         span = slice(part * frames // parts, (part + 1) * frames // parts)
@@ -361,6 +374,18 @@
 def swap(shard, *axes):
     last = 2 ** len(axes) - 1
     return lax.ppermute(shard, axes, [(i, last - i) for i in range(last + 1)])
+
+
+def gather_line(piece):
+    count = lax.axis_size("z")
+    if count <= 4:
+        moved = [
+            lax.ppermute(piece, "z", [(i, i ^ m) for i in range(count)]) for m in range(1, count)
+        ]
+        return jnp.stack([piece] + moved)
+    spread = jnp.broadcast_to(piece[None], (count,) + piece.shape)
+    order = lax.axis_index("z") ^ jnp.arange(count, dtype=jnp.int32)
+    return jnp.take(lax.all_to_all(spread, "z", 0, 0), order, axis=0)
 
 
 def shards(features, seg_lengths):
@@ -405,8 +430,7 @@
     )(partial, tail, total, halo)
     swapped = lax.all_to_all(partial.reshape(tm_count, chunk, B), ("z", "x"), 0, 0)
     summed = jnp.sum(swapped, axis=0)
-    spread = jnp.broadcast_to(summed[None], (line_count, chunk, B))
-    line = lax.all_to_all(spread, "z", 0, 0)
+    line = gather_line(summed)
     held = [line, swap(line, "y"), swap(line, "x"), swap(line, "x", "y")]
     held = held + [swap(part, "c") for part in held]
     return pl.pallas_call(
@@ -423,7 +447,8 @@
             pltpu.VMEM((feat_count, tm_count * chunk, B), F32),
             pltpu.VMEM((width, width), F32),
             pltpu.VMEM((width, width), F32),
-            pltpu.SemaphoreType.DMA((3,)),
+            pltpu.VMEM((width, width), F32),
+            pltpu.SemaphoreType.DMA((5,)),
         ],
         compiler_params=params,
         name="solve",

time: 64.9 us -> 60.5 us (0.932)
  blocking collectives: 26.6 us -> 17.3 us
  starting transfers between devices: 5.15 us -> 9.71 us
  waiting for transfers between devices: 7.46 us -> 9.9 us
  Pallas kernels: 23 us -> 20.9 us
    all_to_all x1 -> x0, blocking collectives: 9.19 us -> none  [shards(): line = lax.all_to_all(spread, 'z', 0, 0)]
    ppermute x0 -> x3, starting transfers between devices: none -> 4.45 us  [gather_line(): lax.ppermute(piece, 'z', [(i, i ^ m) for i in range(count)])]
    ppermute x0 -> x3, waiting for transfers between devices: none -> 2.42 us  [gather_line(): lax.ppermute(piece, 'z', [(i, i ^ m) for i in range(count)])]
    pallas_call x1, Pallas kernels: 19.1 us -> 17.1 us  [shards(): pl.pallas_call(solve_kernel, out_shape=[jax.ShapeDtypeStruct((width // fe...]
  transfers between devices with their start and end apart: 8 -> 11, of which waited for: 6 -> 8; matrix products, arithmetic and copies ran while one was open for 0% -> 0% of each run, Pallas kernels for 6% -> 6%
where the time goes in v3:
time: 60.5 us; the launch traced here: 60.3 us
  Pallas kernels  20.9 us (35%)
  blocking collectives  17.3 us (29%)
  waiting for transfers between devices  9.9 us (16%)
  starting transfers between devices  9.71 us (16%)
  local copies, waits for them, and re-layouts  1.5 us (2%)
  between operations  0.86 us (1%)
    all_to_all x1, blocking collectives, shards(): lax.all_to_all(partial.reshape(tm_count, chunk, B), ('z', 'x'), 0, 0)  17.3 us
    pallas_call x1, Pallas kernels, shards(): pl.pallas_call(solve_kernel, out_shape=[jax.ShapeDtypeStruct((width // fe...  17.1 us
    ppermute x7, waiting for transfers between devices, swap(): return lax.ppermute(shard, axes, [(i, last - i) for i in range(last + 1)])  5.94 us
    ppermute x3, starting transfers between devices, gather_line(): lax.ppermute(piece, 'z', [(i, i ^ m) for i in range(count)])  4.45 us
    ppermute x7, starting transfers between devices, swap(): return lax.ppermute(shard, axes, [(i, last - i) for i in range(last + 1)])  3.84 us
    pallas_call x1, Pallas kernels, shards(): pl.pallas_call(gram_kernel, out_shape=[jax.ShapeDtypeStruct((tm_count * c...  3.57 us
    ppermute x3, waiting for transfers between devices, gather_line(): lax.ppermute(piece, 'z', [(i, i ^ m) for i in range(count)])  2.42 us
    ppermute x1, waiting for transfers between devices, shards(): lax.ppermute(features[:LAG], ('z', 'x'), [(i, i - 1) for i in range(1, tm...  1.54 us
  transfers between devices with their start and end apart: 11, of which 8 were waited for; matrix products, arithmetic and copies ran while one was open for 0% of the time, Pallas kernels for 6%

profile of v3, /device:TPU:0, one launch (start us, length us, event | category | flops | bytes accessed | tf_op | source)
XLA Modules:
  0.0 60.3 jit_solution(13222631627249594235)
XLA Ops:
  0.6 0.8 %slice.3 = bf16[64,512]{1,0:T(8,128)(2,1)S(1)} slice(bf16[2048,512]{1,0:T(8,128)(2,1)} %refs_8_.1), slice={[0:64], [0:512]} | slice | bytes 131072 | tf_op jit(solution)/shard_map/slice | solution.py:396
  1.5 0.0 copy-start
  1.5 1.4 %collective-permute-start = (bf16[64,512]{1,0:T(8,128)(2,1)S(1)}, bf16[64,512]{1,0:T(8,128)(2,1)S(1)}, u32[]{:S(2)}, u32[]{:S(2)}) collective-permute-start(bf16[64,512]{1,0:T(8,128)(2,1)S(1)} %slice.3), channel_id=1, source_target_pairs={{4,0},{8,4},{12,8},{16,12},{20,16},{24,20},{28,24},{5,1},{9,5},{13... | collective-permute-start | bytes 196616 | tf_op jit(solution)/shard_map/ppermute | solution.py:396
  2.9 0.0 copy-start.1
  2.9 0.6 %copy-done.1 = s32[16]{0:T(128)S(1)} copy-done((s32[16]{0:T(128)S(1)}, s32[16]{0:T(128)}, u32[]{:S(2)}) %copy-start.1) | copy-done | bytes 88
  3.6 0.0 copy-start.2
  3.6 3.6 %grams.1 = (f32[640,128]{1,0:T(8,128)S(1)}, bf16[64,512]{1,0:T(8,128)(2,1)S(1)}, f32[8,128]{1,0:T(8,128)S(1)}) custom-call(s32[16]{0:T(128)S(1)} %copy-done.1, bf16[2048,512]{1,0:T(8,128)(2,1)} %refs_8_.1), custom_call_target="tpu_custom_call" | custom-call | flops 603979776 | bytes 2097152 | tf_op jit(solution)/shard_map/grams/pallas_call | solution.py:402
  7.1 1.5 %collective-permute-done.halo_ref.refs_9_ = bf16[64,512]{1,0:T(8,128)(2,1)S(1)} collective-permute-done((bf16[64,512]{1,0:T(8,128)(2,1)S(1)}, bf16[64,512]{1,0:T(8,128)(2,1)S(1)}, u32[]{:S(2)}, u32[]{:S(2)}) %collective-permute-start) | collective-permute-done | bytes 65568 | tf_op jit(solution)/shard_map/ppermute | solution.py:396
  8.7 0.3 edges.1
  9.0 17.3 %all_to_all.5 = f32[8,80,128]{2,1,0:T(8,128)S(1)} all-to-all(f32[8,80,128]{2,1,0:T(8,128)S(1)} %bitcast.5), channel_id=1, replica_groups=mesh['z'=4,'x'=2,'y'=2,'c'=2] {'z','x'}, dimensions={0} | all-to-all | bytes 655360 | tf_op jit(solution)/shard_map/all_to_all | solution.py:431
  26.3 1.5 %collective-permute-start.3 = (f32[80,128]{1,0:T(8,128)S(1)}, f32[80,128]{1,0:T(8,128)S(1)}, u32[]{:S(2)}, u32[]{:S(2)}) collective-permute-start(f32[80,128]{1,0:T(8,128)S(1)} %reduce_sum.9), channel_id=1, source_target_pairs={{0,24},{8,16},{16,8},{24,0},{1,25},{9,17},{17,9},{25,1},{2,26},{10... | collective-permute-start | bytes 122888 | tf_op jit(solution)/shard_map/ppermute | solution.py:383
  27.8 0.8 %collective-permute-start.2 = (f32[80,128]{1,0:T(8,128)S(1)}, f32[80,128]{1,0:T(8,128)S(1)}, u32[]{:S(2)}, u32[]{:S(2)}) collective-permute-start(f32[80,128]{1,0:T(8,128)S(1)} %reduce_sum.9), channel_id=1, source_target_pairs={{0,16},{8,24},{16,0},{24,8},{1,17},{9,25},{17,1},{25,9},{2,18},{10... | collective-permute-start | bytes 122888 | tf_op jit(solution)/shard_map/ppermute | solution.py:383
  28.6 2.2 %collective-permute-start.1 = (f32[80,128]{1,0:T(8,128)S(1)}, f32[80,128]{1,0:T(8,128)S(1)}, u32[]{:S(2)}, u32[]{:S(2)}) collective-permute-start(f32[80,128]{1,0:T(8,128)S(1)} %reduce_sum.9), channel_id=1, source_target_pairs={{0,8},{8,0},{16,24},{24,16},{1,9},{9,1},{17,25},{25,17},{2,10},{10... | collective-permute-start | bytes 122888 | tf_op jit(solution)/shard_map/ppermute | solution.py:383
  30.8 1.4 %collective-permute-done.3 = f32[80,128]{1,0:T(8,128)S(1)} collective-permute-done((f32[80,128]{1,0:T(8,128)S(1)}, f32[80,128]{1,0:T(8,128)S(1)}, u32[]{:S(2)}, u32[]{:S(2)}) %collective-permute-start.3) | collective-permute-done | bytes 40992 | tf_op jit(solution)/shard_map/ppermute | solution.py:383
  32.2 1.0 %collective-permute-done.2 = f32[80,128]{1,0:T(8,128)S(1)} collective-permute-done((f32[80,128]{1,0:T(8,128)S(1)}, f32[80,128]{1,0:T(8,128)S(1)}, u32[]{:S(2)}, u32[]{:S(2)}) %collective-permute-start.2) | collective-permute-done | bytes 40992 | tf_op jit(solution)/shard_map/ppermute | solution.py:383
  33.2 0.0 collective-permute-done.1
  33.2 2.0 %collective-permute-start.6 = (f32[4,80,128]{2,1,0:T(8,128)S(1)}, f32[4,80,128]{2,1,0:T(8,128)S(1)}, u32[]{:S(2)}, u32[]{:S(2)}) collective-permute-start(f32[4,80,128]{2,1,0:T(8,128)S(1)} %pad_maximum_fusion.refs_0_), channel_id=1, source_target_pairs={{0,6},{2,4},{4,2},{6,0},{1,7},{3,5},{5,3},{7,1},{8,14},{10,12},{12... | collective-permute-start | bytes 491528 | tf_op jit(solution)/shard_map/ppermute | solution.py:376
  35.2 1.1 %collective-permute-start.5 = (f32[4,80,128]{2,1,0:T(8,128)S(1)}, f32[4,80,128]{2,1,0:T(8,128)S(1)}, u32[]{:S(2)}, u32[]{:S(2)}) collective-permute-start(f32[4,80,128]{2,1,0:T(8,128)S(1)} %pad_maximum_fusion.refs_0_), channel_id=1, source_target_pairs={{0,4},{4,0},{1,5},{5,1},{2,6},{6,2},{3,7},{7,3},{8,12},{12,8},{9,1... | collective-permute-start | bytes 491528 | tf_op jit(solution)/shard_map/ppermute | solution.py:376
  36.3 0.5 collective-permute-start.4
  36.8 0.0 collective-permute-start.7
  36.8 2.7 %collective-permute-done.6.refs_3_ = f32[4,80,128]{2,1,0:T(8,128)S(1)} collective-permute-done((f32[4,80,128]{2,1,0:T(8,128)S(1)}, f32[4,80,128]{2,1,0:T(8,128)S(1)}, u32[]{:S(2)}, u32[]{:S(2)}) %collective-permute-start.6) | collective-permute-done | bytes 163872 | tf_op jit(solution)/shard_map/ppermute | solution.py:376
  39.5 0.0 collective-permute-start.10
  39.5 1.9 %collective-permute-done.5.refs_2_ = f32[4,80,128]{2,1,0:T(8,128)S(1)} collective-permute-done((f32[4,80,128]{2,1,0:T(8,128)S(1)}, f32[4,80,128]{2,1,0:T(8,128)S(1)}, u32[]{:S(2)}, u32[]{:S(2)}) %collective-permute-start.5) | collective-permute-done | bytes 163872 | tf_op jit(solution)/shard_map/ppermute | solution.py:376
  41.4 0.0 collective-permute-start.9
  41.4 0.2 collective-permute-done.4.refs_1_
  41.6 0.3 collective-permute-start.8
  41.9 0.0 collective-permute-done.7.refs_4_
  41.9 0.0 collective-permute-done.10.refs_7_
  41.9 0.9 %collective-permute-done.9.refs_6_ = f32[4,80,128]{2,1,0:T(8,128)S(1)} collective-permute-done((f32[4,80,128]{2,1,0:T(8,128)S(1)}, f32[4,80,128]{2,1,0:T(8,128)S(1)}, u32[]{:S(2)}, u32[]{:S(2)}) %collective-permute-start.9) | collective-permute-done | bytes 163872 | tf_op jit(solution)/shard_map/ppermute | solution.py:376
  42.8 0.2 collective-permute-done.8.refs_5_
  43.0 0.0 copy-done
  43.0 0.0 copy-done.2
  43.0 17.1 %solve.1 = (f32[128,512]{1,0:T(8,128)}, f32[32,2048]{1,0:T(8,128)}) custom-call(s32[16]{0:T(128)S(1)} %copy-done.2, f32[4,80,128]{2,1,0:T(8,128)S(1)} %pad_maximum_fusion.refs_0_, f32[4,80,128]{2,1,0:T(8,128)S(1)} %collective-permute-done.4.refs_1_, f32[4,80,128]{2,1,0:T(8,128)S(1)} %collective-permute-done.5.refs_2_, ...), custom_call_target="tpu_custom_call" | custom-call | tf_op jit(solution)/shard_map/solve/pallas_call | solution.py:436
  (2 shorter events, 0.0 us)
Async XLA Ops:
  1.5 41.6 %copy-start = (bf16[2048,512]{1,0:T(8,128)(2,1)S(1)}, bf16[2048,512]{1,0:T(8,128)(2,1)}, u32[]{:S(2)}) copy-start(bf16[2048,512]{1,0:T(8,128)(2,1)} %refs_8_.1) | copy-start | bytes 6291460
  1.5 7.2 %collective-permute-start = (bf16[64,512]{1,0:T(8,128)(2,1)S(1)}, bf16[64,512]{1,0:T(8,128)(2,1)S(1)}, u32[]{:S(2)}, u32[]{:S(2)}) collective-permute-start(bf16[64,512]{1,0:T(8,128)(2,1)S(1)} %slice.3), channel_id=1, source_target_pairs={{4,0},{8,4},{12,8},{16,12},{20,16},{24,20},{28,24},{5,1},{9,5},{13... | collective-permute-start | bytes 196616 | tf_op jit(solution)/shard_map/ppermute | solution.py:396
  2.9 0.7 %copy-start.1 = (s32[16]{0:T(128)S(1)}, s32[16]{0:T(128)}, u32[]{:S(2)}) copy-start(s32[16]{0:T(128)} %seg_ref.1) | copy-start | bytes 196
  3.6 39.5 %copy-start.2 = (s32[16]{0:T(128)S(1)}, s32[16]{0:T(128)}, u32[]{:S(2)}) copy-start(s32[16]{0:T(128)} %seg_ref.1) | copy-start | bytes 196
  26.3 5.9 %collective-permute-start.3 = (f32[80,128]{1,0:T(8,128)S(1)}, f32[80,128]{1,0:T(8,128)S(1)}, u32[]{:S(2)}, u32[]{:S(2)}) collective-permute-start(f32[80,128]{1,0:T(8,128)S(1)} %reduce_sum.9), channel_id=1, source_target_pairs={{0,24},{8,16},{16,8},{24,0},{1,25},{9,17},{17,9},{25,1},{2,26},{10... | collective-permute-start | bytes 122888 | tf_op jit(solution)/shard_map/ppermute | solution.py:383
  27.8 5.4 %collective-permute-start.2 = (f32[80,128]{1,0:T(8,128)S(1)}, f32[80,128]{1,0:T(8,128)S(1)}, u32[]{:S(2)}, u32[]{:S(2)}) collective-permute-start(f32[80,128]{1,0:T(8,128)S(1)} %reduce_sum.9), channel_id=1, source_target_pairs={{0,16},{8,24},{16,0},{24,8},{1,17},{9,25},{17,1},{25,9},{2,18},{10... | collective-permute-start | bytes 122888 | tf_op jit(solution)/shard_map/ppermute | solution.py:383
  28.6 4.6 %collective-permute-start.1 = (f32[80,128]{1,0:T(8,128)S(1)}, f32[80,128]{1,0:T(8,128)S(1)}, u32[]{:S(2)}, u32[]{:S(2)}) collective-permute-start(f32[80,128]{1,0:T(8,128)S(1)} %reduce_sum.9), channel_id=1, source_target_pairs={{0,8},{8,0},{16,24},{24,16},{1,9},{9,1},{17,25},{25,17},{2,10},{10... | collective-permute-start | bytes 122888 | tf_op jit(solution)/shard_map/ppermute | solution.py:383
  33.2 6.3 %collective-permute-start.6 = (f32[4,80,128]{2,1,0:T(8,128)S(1)}, f32[4,80,128]{2,1,0:T(8,128)S(1)}, u32[]{:S(2)}, u32[]{:S(2)}) collective-permute-start(f32[4,80,128]{2,1,0:T(8,128)S(1)} %pad_maximum_fusion.refs_0_), channel_id=1, source_target_pairs={{0,6},{2,4},{4,2},{6,0},{1,7},{3,5},{5,3},{7,1},{8,14},{10,12},{12... | collective-permute-start | bytes 491528 | tf_op jit(solution)/shard_map/ppermute | solution.py:376
  35.2 6.2 %collective-permute-start.5 = (f32[4,80,128]{2,1,0:T(8,128)S(1)}, f32[4,80,128]{2,1,0:T(8,128)S(1)}, u32[]{:S(2)}, u32[]{:S(2)}) collective-permute-start(f32[4,80,128]{2,1,0:T(8,128)S(1)} %pad_maximum_fusion.refs_0_), channel_id=1, source_target_pairs={{0,4},{4,0},{1,5},{5,1},{2,6},{6,2},{3,7},{7,3},{8,12},{12,8},{9,1... | collective-permute-start | bytes 491528 | tf_op jit(solution)/shard_map/ppermute | solution.py:376
  36.3 5.3 %collective-permute-start.4 = (f32[4,80,128]{2,1,0:T(8,128)S(1)}, f32[4,80,128]{2,1,0:T(8,128)S(1)}, u32[]{:S(2)}, u32[]{:S(2)}) collective-permute-start(f32[4,80,128]{2,1,0:T(8,128)S(1)} %pad_maximum_fusion.refs_0_), channel_id=1, source_target_pairs={{0,2},{2,0},{1,3},{3,1},{4,6},{6,4},{5,7},{7,5},{8,10},{10,8},{9,1... | collective-permute-start | bytes 491528 | tf_op jit(solution)/shard_map/ppermute | solution.py:376
  36.8 5.1 %collective-permute-start.7 = (f32[4,80,128]{2,1,0:T(8,128)S(1)}, f32[4,80,128]{2,1,0:T(8,128)S(1)}, u32[]{:S(2)}, u32[]{:S(2)}) collective-permute-start(f32[4,80,128]{2,1,0:T(8,128)S(1)} %pad_maximum_fusion.refs_0_), channel_id=1, source_target_pairs={{0,1},{1,0},{2,3},{3,2},{4,5},{5,4},{6,7},{7,6},{8,9},{9,8},{10,11... | collective-permute-start | bytes 491528 | tf_op jit(solution)/shard_map/ppermute | solution.py:376
  39.5 2.4 %collective-permute-start.10 = (f32[4,80,128]{2,1,0:T(8,128)S(1)}, f32[4,80,128]{2,1,0:T(8,128)S(1)}, u32[]{:S(2)}, u32[]{:S(2)}) collective-permute-start(f32[4,80,128]{2,1,0:T(8,128)S(1)} %collective-permute-done.6.refs_3_), channel_id=1, source_target_pairs={{0,1},{1,0},{2,3},{3,2},{4,5},{5,4},{6,7},{7,6},{8,9},{9,8},{10,11... | collective-permute-start | bytes 491528 | tf_op jit(solution)/shard_map/ppermute | solution.py:376
  41.4 1.4 %collective-permute-start.9 = (f32[4,80,128]{2,1,0:T(8,128)S(1)}, f32[4,80,128]{2,1,0:T(8,128)S(1)}, u32[]{:S(2)}, u32[]{:S(2)}) collective-permute-start(f32[4,80,128]{2,1,0:T(8,128)S(1)} %collective-permute-done.5.refs_2_), channel_id=1, source_target_pairs={{0,1},{1,0},{2,3},{3,2},{4,5},{5,4},{6,7},{7,6},{8,9},{9,8},{10,11... | collective-permute-start | bytes 491528 | tf_op jit(solution)/shard_map/ppermute | solution.py:376
  41.6 1.4 %collective-permute-start.8 = (f32[4,80,128]{2,1,0:T(8,128)S(1)}, f32[4,80,128]{2,1,0:T(8,128)S(1)}, u32[]{:S(2)}, u32[]{:S(2)}) collective-permute-start(f32[4,80,128]{2,1,0:T(8,128)S(1)} %collective-permute-done.4.refs_1_), channel_id=1, source_target_pairs={{0,1},{1,0},{2,3},{3,2},{4,5},{5,4},{6,7},{7,6},{8,9},{9,8},{10,11... | collective-permute-start | bytes 491528 | tf_op jit(solution)/shard_map/ppermute | solution.py:376

commit v4 on v3

--- a/solution.py
+++ b/solution.py
@@ -11,6 +11,8 @@
 HIGHEST = lax.Precision.HIGHEST
 B = 128
 PICKED = 2 * B + B // 2
+SIDE = PICKED - B
+PACKED = 2 * SIDE + B + 8
 LOADS = 4
 AHEAD = 2
 F32 = jnp.float32
@@ -76,16 +78,14 @@
         + lax.broadcasted_iota(jnp.int32, (groups, B), 1)
     )
     ahead = valid_at(seg_ref, moments)
-    behind = jnp.where(moments >= LAG, valid_at(seg_ref, moments - LAG), 0.0)
-    local_behind = jnp.where(moments - first >= LAG, behind, 0.0)
-    stacked = jnp.concatenate(
-        [ahead, local_behind, ahead + behind, jnp.zeros((B - 3 * groups, B), F32)], axis=0
-    )
-    columns = stacked.T
+    start = jnp.where(moments[:8] >= LAG, valid_at(seg_ref, moments[:8] - LAG), 0.0)
+    columns = jnp.concatenate([ahead, start, jnp.zeros((B - groups - 8, B), F32)], axis=0).T
 
     def weight(row):
         return jnp.broadcast_to(columns[:, row : row + 1], (B, B))
 
+    weights = [weight(g) for g in range(groups)]
+    first_behind = weight(groups)[:LAG]
     total = jnp.zeros((8, B), F32)
     half = B - LAG
     copies[0].wait()
@@ -107,14 +107,17 @@
                 earlier = jnp.concatenate(
                     [jnp.zeros((LAG, B), F32), x_ref[0:half, cols].astype(F32)], axis=0
                 )
-            weighted = own * weight(2 * groups + g)
+            before = weights[g - 1][half:] if g > 0 else jnp.zeros((LAG, B), F32)
+            behind = jnp.concatenate([before, weights[g][:half]], axis=0)
+            both = jnp.concatenate([before if g > 0 else first_behind, weights[g][:half]], axis=0)
+            weighted = own * (weights[g] + both)
             z_ref[low : low + B, 0:B] = weighted.astype(BF16)
-            z_ref[low : low + B, B : 2 * B] = (later * weight(g)).astype(BF16)
-            z_ref[low : low + B, 2 * B : 3 * B] = (earlier * weight(groups + g)).astype(BF16)
+            z_ref[low : low + B, B : 2 * B] = (later * weights[g]).astype(BF16)
+            z_ref[low : low + B, 2 * B : 3 * B] = (earlier * behind).astype(BF16)
             for part in range(B // 8):
                 total = total + weighted[8 * part : 8 * part + 8]
     last = x_ref[frames - LAG : frames, :].astype(F32)
-    tail_weight = jnp.concatenate([weight(groups - 1)[half:]] * (last.shape[1] // B), axis=1)
+    tail_weight = jnp.concatenate([weights[groups - 1][half:]] * (last.shape[1] // B), axis=1)
     tail_ref[...] = (last * tail_weight).astype(BF16)
     total_ref[...] = jnp.broadcast_to(jnp.sum(total, axis=0, keepdims=True), (8, B))
     for back in range(3):
@@ -124,14 +127,10 @@
                 out_ref[base + back * B : base + (back + 1) * B, :] = gram
             else:
                 out_ref[base + 2 * B : base + PICKED, :] = half_block(gram)
-    if out_ref.shape[0] > 2 * PICKED:
-        out_ref[2 * PICKED :, :] = jnp.zeros((out_ref.shape[0] - 2 * PICKED, B), F32)
-
-
-def sum_places():
-    row = lax.broadcasted_iota(jnp.int32, (B, B), 0)
-    lane = lax.broadcasted_iota(jnp.int32, (B, B), 1)
-    return row, lane, ((row == B - 1) & (lane < B - 1)) | ((row == B - 2) & (lane == 0))
+
+
+def square_places():
+    return lax.broadcasted_iota(jnp.int32, (B, B), 0), lax.broadcasted_iota(jnp.int32, (B, B), 1)
 
 
 def edge_kernel(part_ref, tail_ref, total_ref, halo_ref, out_ref):
@@ -141,18 +140,18 @@
         + contract(halo_ref[:, own_block(back)], tail_ref[:, cols])
         for back in range(3)
     ]
-    lows = [PICKED, PICKED + B, PICKED + 2 * B]
-    out_ref[:PICKED, :] = part_ref[:PICKED, :]
-    row, lane, places = sum_places()
-    total = jnp.broadcast_to(total_ref[0:1, :], (B, B))
-    total = jnp.where(row == B - 1, total, jnp.broadcast_to(total[:, B - 1 :], (B, B)))
-    own = part_ref[lows[0] : lows[1], :] + extra[0]
-    out_ref[lows[0] : lows[1], :] = jnp.where(places, total, own)
-    out_ref[lows[1] : lows[2], :] = part_ref[lows[1] : lows[2], :] + extra[1]
-    high = lows[2] + B // 2
-    out_ref[lows[2] : high, :] = part_ref[lows[2] : high, :] + half_block(extra[2])
-    if out_ref.shape[0] > high:
-        out_ref[high:, :] = part_ref[high:, :]
+    out_ref[:SIDE, :] = part_ref[B:PICKED, :]
+    out_ref[SIDE : SIDE + B, :] = part_ref[PICKED + B : PICKED + 2 * B, :] + extra[1]
+    out_ref[SIDE + B : 2 * SIDE, :] = part_ref[PICKED + 2 * B :, :] + half_block(extra[2])
+    row, lane = square_places()
+    own = part_ref[PICKED : PICKED + B, :] + extra[0]
+    out_ref[2 * SIDE : 2 * SIDE + B, :] = jnp.where(lane >= row, part_ref[:B, :], own)
+    diag = jnp.sum(jnp.where(lane == row, own, 0.0), axis=0, keepdims=True)
+    last = lax.broadcasted_iota(jnp.int32, (8, B), 0)
+    last = jnp.where(last == 0, diag, jnp.where(last == 1, total_ref[...], 0.0))
+    out_ref[2 * SIDE + B : PACKED, :] = last
+    if out_ref.shape[0] > PACKED:
+        out_ref[PACKED:, :] = jnp.zeros((out_ref.shape[0] - PACKED, B), F32)
 
 
 def across(tile, lane):
@@ -241,24 +240,25 @@
     pairs = lax.fori_loop(0, seg_ref.shape[0], add_pairs, jnp.int32(0), unroll=True)
     ones = jnp.ones((8, B), F32)
     inv_pairs = (1.0 / (ones * (2.0 * pairs.astype(F32))))[0:1, :]
-    row, lane, places = sum_places()
-    mean_row = []
-    for f in range(n):
-        packed = flat_ref[f, PICKED : PICKED + B, :]
-        sums = jnp.where(
-            lane[:1] < B - 1, packed[B - 1 :], jnp.broadcast_to(packed[B - 2 : B - 1, :1], (1, B))
-        )
-        mean_row.append(sums * inv_pairs)
-        flat_ref[f, PICKED : PICKED + B, :] = jnp.where(places, packed.T, packed)
+    row, lane = square_places()
+    low = 2 * SIDE + B
+    mean_row = [flat_ref[f, low + 1 : low + 2, :] * inv_pairs for f in range(n)]
     mean_col = [jnp.broadcast_to(mean_row[f], (B, B)).T for f in range(n)]
+
+    squares = [flat_ref[f, 2 * SIDE : 2 * SIDE + B, :] for f in range(n)]
+    turned = [square.T for square in squares]
 
     def summed(base, i, j):
         back = (j - i) % n
-        if back < 2:
-            return flat_ref[j, base + back * B : base + (back + 1) * B, :]
+        if back == 0 and base == 0:
+            return jnp.where(lane >= row, squares[i], turned[i])
+        if back == 0:
+            diag = jnp.broadcast_to(flat_ref[i, 2 * SIDE + B : 2 * SIDE + B + 1, :], (B, B))
+            return jnp.where(lane == row, diag, jnp.where(lane < row, squares[i], turned[i]))
+        if back == 1:
+            return flat_ref[j, base : base + B, :]
         if i < j and back == 2:
-            low = base + 2 * B
-            pieces = [flat_ref[f, low : low + B // 2, :] for f in (i, j)]
+            pieces = [flat_ref[f, base + B : base + SIDE, :] for f in (i, j)]
             return jnp.concatenate(pieces, axis=0)
         return summed(base, j, i).T
 
@@ -287,7 +287,7 @@
         inv = leaf_inverse(upper[k, k])
         if k == 0:
             for i in range(n):
-                lagged[i] = jnp.concatenate([moment(PICKED, i, j) for j in range(n)], axis=1)
+                lagged[i] = jnp.concatenate([moment(SIDE, i, j) for j in range(n)], axis=1)
         rest = range(k + 1, n)
         if rest:
             near = dot_nn(inv, upper[k, k + 1])
@@ -394,7 +394,7 @@
     tm_count = line_count * lax.axis_size("x")
     feat_count = lax.axis_size("y") * lax.axis_size("c")
     halo = lax.ppermute(features[:LAG], ("z", "x"), [(i, i - 1) for i in range(1, tm_count)])
-    chunk = -(-2 * PICKED // (8 * tm_count)) * 8
+    chunk = -(-PACKED // (8 * tm_count)) * 8
     vmem = pl.BlockSpec(memory_space=pltpu.VMEM)
     smem = pl.BlockSpec(memory_space=pltpu.SMEM)
     params = pltpu.CompilerParams(vmem_limit_bytes=VMEM_LIMIT)
@@ -402,7 +402,7 @@
     partial, tail, total = pl.pallas_call(
         gram_kernel,
         out_shape=[
-            jax.ShapeDtypeStruct((tm_count * chunk, B), F32),
+            jax.ShapeDtypeStruct((2 * PICKED, B), F32),
             jax.ShapeDtypeStruct((LAG, width), BF16),
             jax.ShapeDtypeStruct((8, B), F32),
         ],

time: 60.5 us -> 58.9 us (0.974)
  blocking collectives: 17.3 us -> 15.9 us
  waiting for transfers between devices: 9.9 us -> 10.7 us
  Pallas kernels: 20.9 us -> 20.2 us
    all_to_all x1, blocking collectives: 17.3 us -> 15.9 us  [shards(): lax.all_to_all(partial.reshape(tm_count, chunk, B), ('z', 'x'), 0, 0)]
    ppermute x1, waiting for transfers between devices: 1.54 us -> 2.4 us  [shards(): lax.ppermute(features[:LAG], ('z', 'x'), [(i, i - 1) for i in range(1, tm...]
    pallas_call x1, Pallas kernels: 3.57 us -> 2.72 us  [shards(): pl.pallas_call(gram_kernel, out_shape=[jax.ShapeDtypeStruct((2 * PICKED,...]
  transfers between devices with their start and end apart: 11 -> 11, of which waited for: 8 -> 9; matrix products, arithmetic and copies ran while one was open for 0% -> 0% of each run, Pallas kernels for 6% -> 5%
where the time goes in v4:
time: 58.9 us; the launch traced here: 58.6 us
  Pallas kernels  20.2 us (34%)
  blocking collectives  15.9 us (27%)
  waiting for transfers between devices  10.7 us (18%)
  starting transfers between devices  9.49 us (16%)
  local copies, waits for them, and re-layouts  1.5 us (3%)
  between operations  0.84 us (1%)
    pallas_call x1, Pallas kernels, shards(): pl.pallas_call(solve_kernel, out_shape=[jax.ShapeDtypeStruct((width // fe...  17.2 us
    all_to_all x1, blocking collectives, shards(): lax.all_to_all(partial.reshape(tm_count, chunk, B), ('z', 'x'), 0, 0)  15.9 us
    ppermute x7, waiting for transfers between devices, swap(): return lax.ppermute(shard, axes, [(i, last - i) for i in range(last + 1)])  5.96 us
    ppermute x3, starting transfers between devices, gather_line(): lax.ppermute(piece, 'z', [(i, i ^ m) for i in range(count)])  4.45 us
    ppermute x7, starting transfers between devices, swap(): return lax.ppermute(shard, axes, [(i, last - i) for i in range(last + 1)])  3.63 us
    pallas_call x1, Pallas kernels, shards(): pl.pallas_call(gram_kernel, out_shape=[jax.ShapeDtypeStruct((2 * PICKED,...  2.72 us
    ppermute x1, waiting for transfers between devices, shards(): lax.ppermute(features[:LAG], ('z', 'x'), [(i, i - 1) for i in range(1, tm...  2.4 us
    ppermute x3, waiting for transfers between devices, gather_line(): lax.ppermute(piece, 'z', [(i, i ^ m) for i in range(count)])  2.33 us
  transfers between devices with their start and end apart: 11, of which 9 were waited for; matrix products, arithmetic and copies ran while one was open for 0% of the time, Pallas kernels for 5%

profile of v4, /device:TPU:0, one launch (start us, length us, event | category | flops | bytes accessed | tf_op | source)
XLA Modules:
  0.0 58.6 jit_solution(6340142297337418392)
XLA Ops:
  0.6 0.8 %slice.3 = bf16[64,512]{1,0:T(8,128)(2,1)S(1)} slice(bf16[2048,512]{1,0:T(8,128)(2,1)} %refs_8_.1), slice={[0:64], [0:512]} | slice | bytes 131072 | tf_op jit(solution)/shard_map/slice | solution.py:396
  1.5 0.0 copy-start
  1.5 1.4 %collective-permute-start = (bf16[64,512]{1,0:T(8,128)(2,1)S(1)}, bf16[64,512]{1,0:T(8,128)(2,1)S(1)}, u32[]{:S(2)}, u32[]{:S(2)}) collective-permute-start(bf16[64,512]{1,0:T(8,128)(2,1)S(1)} %slice.3), channel_id=1, source_target_pairs={{4,0},{8,4},{12,8},{16,12},{20,16},{24,20},{28,24},{5,1},{9,5},{13... | collective-permute-start | bytes 196616 | tf_op jit(solution)/shard_map/ppermute | solution.py:396
  2.9 0.0 copy-start.1
  2.9 0.6 %copy-done.1 = s32[16]{0:T(128)S(1)} copy-done((s32[16]{0:T(128)S(1)}, s32[16]{0:T(128)}, u32[]{:S(2)}) %copy-start.1) | copy-done | bytes 88
  3.6 0.0 copy-start.2
  3.6 2.7 %grams.1 = (f32[640,128]{1,0:T(8,128)S(1)}, bf16[64,512]{1,0:T(8,128)(2,1)S(1)}, f32[8,128]{1,0:T(8,128)S(1)}) custom-call(s32[16]{0:T(128)S(1)} %copy-done.1, bf16[2048,512]{1,0:T(8,128)(2,1)} %refs_8_.1), custom_call_target="tpu_custom_call" | custom-call | flops 603979776 | bytes 2097152 | tf_op jit(solution)/shard_map/grams/pallas_call | solution.py:402
  6.3 2.4 %collective-permute-done.halo_ref.refs_9_ = bf16[64,512]{1,0:T(8,128)(2,1)S(1)} collective-permute-done((bf16[64,512]{1,0:T(8,128)(2,1)S(1)}, bf16[64,512]{1,0:T(8,128)(2,1)S(1)}, u32[]{:S(2)}, u32[]{:S(2)}) %collective-permute-start) | collective-permute-done | bytes 65568 | tf_op jit(solution)/shard_map/ppermute | solution.py:396
  8.7 0.3 edges.1
  9.0 15.9 %all_to_all.5 = f32[8,72,128]{2,1,0:T(8,128)S(1)} all-to-all(f32[8,72,128]{2,1,0:T(8,128)S(1)} %bitcast.5), channel_id=1, replica_groups=mesh['z'=4,'x'=2,'y'=2,'c'=2] {'z','x'}, dimensions={0} | all-to-all | bytes 589824 | tf_op jit(solution)/shard_map/all_to_all | solution.py:431
  24.9 1.5 %collective-permute-start.3 = (f32[72,128]{1,0:T(8,128)S(1)}, f32[72,128]{1,0:T(8,128)S(1)}, u32[]{:S(2)}, u32[]{:S(2)}) collective-permute-start(f32[72,128]{1,0:T(8,128)S(1)} %reduce_sum.9), channel_id=1, source_target_pairs={{0,24},{8,16},{16,8},{24,0},{1,25},{9,17},{17,9},{25,1},{2,26},{10... | collective-permute-start | bytes 110600 | tf_op jit(solution)/shard_map/ppermute | solution.py:383
  26.4 0.7 %collective-permute-start.2 = (f32[72,128]{1,0:T(8,128)S(1)}, f32[72,128]{1,0:T(8,128)S(1)}, u32[]{:S(2)}, u32[]{:S(2)}) collective-permute-start(f32[72,128]{1,0:T(8,128)S(1)} %reduce_sum.9), channel_id=1, source_target_pairs={{0,16},{8,24},{16,0},{24,8},{1,17},{9,25},{17,1},{25,9},{2,18},{10... | collective-permute-start | bytes 110600 | tf_op jit(solution)/shard_map/ppermute | solution.py:383
  27.1 2.3 %collective-permute-start.1 = (f32[72,128]{1,0:T(8,128)S(1)}, f32[72,128]{1,0:T(8,128)S(1)}, u32[]{:S(2)}, u32[]{:S(2)}) collective-permute-start(f32[72,128]{1,0:T(8,128)S(1)} %reduce_sum.9), channel_id=1, source_target_pairs={{0,8},{8,0},{16,24},{24,16},{1,9},{9,1},{17,25},{25,17},{2,10},{10... | collective-permute-start | bytes 110600 | tf_op jit(solution)/shard_map/ppermute | solution.py:383
  29.4 1.4 %collective-permute-done.3 = f32[72,128]{1,0:T(8,128)S(1)} collective-permute-done((f32[72,128]{1,0:T(8,128)S(1)}, f32[72,128]{1,0:T(8,128)S(1)}, u32[]{:S(2)}, u32[]{:S(2)}) %collective-permute-start.3) | collective-permute-done | bytes 36896 | tf_op jit(solution)/shard_map/ppermute | solution.py:383
  30.7 0.9 %collective-permute-done.2 = f32[72,128]{1,0:T(8,128)S(1)} collective-permute-done((f32[72,128]{1,0:T(8,128)S(1)}, f32[72,128]{1,0:T(8,128)S(1)}, u32[]{:S(2)}, u32[]{:S(2)}) %collective-permute-start.2) | collective-permute-done | bytes 36896 | tf_op jit(solution)/shard_map/ppermute | solution.py:383
  31.6 0.1 collective-permute-done.1
  31.7 1.8 %collective-permute-start.6 = (f32[4,72,128]{2,1,0:T(8,128)S(1)}, f32[4,72,128]{2,1,0:T(8,128)S(1)}, u32[]{:S(2)}, u32[]{:S(2)}) collective-permute-start(f32[4,72,128]{2,1,0:T(8,128)S(1)} %pad_maximum_fusion.refs_0_), channel_id=1, source_target_pairs={{0,6},{2,4},{4,2},{6,0},{1,7},{3,5},{5,3},{7,1},{8,14},{10,12},{12... | collective-permute-start | bytes 442376 | tf_op jit(solution)/shard_map/ppermute | solution.py:376
  33.5 1.3 %collective-permute-start.5 = (f32[4,72,128]{2,1,0:T(8,128)S(1)}, f32[4,72,128]{2,1,0:T(8,128)S(1)}, u32[]{:S(2)}, u32[]{:S(2)}) collective-permute-start(f32[4,72,128]{2,1,0:T(8,128)S(1)} %pad_maximum_fusion.refs_0_), channel_id=1, source_target_pairs={{0,4},{4,0},{1,5},{5,1},{2,6},{6,2},{3,7},{7,3},{8,12},{12,8},{9,1... | collective-permute-start | bytes 442376 | tf_op jit(solution)/shard_map/ppermute | solution.py:376
  34.8 0.5 collective-permute-start.4
  35.3 0.0 collective-permute-start.7
  35.3 2.5 %collective-permute-done.6.refs_3_ = f32[4,72,128]{2,1,0:T(8,128)S(1)} collective-permute-done((f32[4,72,128]{2,1,0:T(8,128)S(1)}, f32[4,72,128]{2,1,0:T(8,128)S(1)}, u32[]{:S(2)}, u32[]{:S(2)}) %collective-permute-start.6) | collective-permute-done | bytes 147488 | tf_op jit(solution)/shard_map/ppermute | solution.py:376
  37.8 0.0 collective-permute-start.10
  37.8 1.7 %collective-permute-done.5.refs_2_ = f32[4,72,128]{2,1,0:T(8,128)S(1)} collective-permute-done((f32[4,72,128]{2,1,0:T(8,128)S(1)}, f32[4,72,128]{2,1,0:T(8,128)S(1)}, u32[]{:S(2)}, u32[]{:S(2)}) %collective-permute-start.5) | collective-permute-done | bytes 147488 | tf_op jit(solution)/shard_map/ppermute | solution.py:376
  39.5 0.0 collective-permute-start.9
  39.5 0.4 collective-permute-done.4.refs_1_
  39.9 0.1 collective-permute-start.8
  40.0 0.0 collective-permute-done.7.refs_4_
  40.0 0.0 collective-permute-done.10.refs_7_
  40.0 0.9 %collective-permute-done.9.refs_6_ = f32[4,72,128]{2,1,0:T(8,128)S(1)} collective-permute-done((f32[4,72,128]{2,1,0:T(8,128)S(1)}, f32[4,72,128]{2,1,0:T(8,128)S(1)}, u32[]{:S(2)}, u32[]{:S(2)}) %collective-permute-start.9) | collective-permute-done | bytes 147488 | tf_op jit(solution)/shard_map/ppermute | solution.py:376
  40.9 0.4 collective-permute-done.8.refs_5_
  41.3 0.0 copy-done
  41.3 0.0 copy-done.2
  41.3 17.2 %solve.1 = (f32[128,512]{1,0:T(8,128)}, f32[32,2048]{1,0:T(8,128)}) custom-call(s32[16]{0:T(128)S(1)} %copy-done.2, f32[4,72,128]{2,1,0:T(8,128)S(1)} %pad_maximum_fusion.refs_0_, f32[4,72,128]{2,1,0:T(8,128)S(1)} %collective-permute-done.4.refs_1_, f32[4,72,128]{2,1,0:T(8,128)S(1)} %collective-permute-done.5.refs_2_, ...), custom_call_target="tpu_custom_call" | custom-call | tf_op jit(solution)/shard_map/solve/pallas_call | solution.py:436
  (2 shorter events, 0.0 us)
Async XLA Ops:
  1.5 39.8 %copy-start = (bf16[2048,512]{1,0:T(8,128)(2,1)S(1)}, bf16[2048,512]{1,0:T(8,128)(2,1)}, u32[]{:S(2)}) copy-start(bf16[2048,512]{1,0:T(8,128)(2,1)} %refs_8_.1) | copy-start | bytes 6291460
  1.5 7.2 %collective-permute-start = (bf16[64,512]{1,0:T(8,128)(2,1)S(1)}, bf16[64,512]{1,0:T(8,128)(2,1)S(1)}, u32[]{:S(2)}, u32[]{:S(2)}) collective-permute-start(bf16[64,512]{1,0:T(8,128)(2,1)S(1)} %slice.3), channel_id=1, source_target_pairs={{4,0},{8,4},{12,8},{16,12},{20,16},{24,20},{28,24},{5,1},{9,5},{13... | collective-permute-start | bytes 196616 | tf_op jit(solution)/shard_map/ppermute | solution.py:396
  2.9 0.7 %copy-start.1 = (s32[16]{0:T(128)S(1)}, s32[16]{0:T(128)}, u32[]{:S(2)}) copy-start(s32[16]{0:T(128)} %seg_ref.1) | copy-start | bytes 196
  3.6 37.8 %copy-start.2 = (s32[16]{0:T(128)S(1)}, s32[16]{0:T(128)}, u32[]{:S(2)}) copy-start(s32[16]{0:T(128)} %seg_ref.1) | copy-start | bytes 196
  24.9 5.8 %collective-permute-start.3 = (f32[72,128]{1,0:T(8,128)S(1)}, f32[72,128]{1,0:T(8,128)S(1)}, u32[]{:S(2)}, u32[]{:S(2)}) collective-permute-start(f32[72,128]{1,0:T(8,128)S(1)} %reduce_sum.9), channel_id=1, source_target_pairs={{0,24},{8,16},{16,8},{24,0},{1,25},{9,17},{17,9},{25,1},{2,26},{10... | collective-permute-start | bytes 110600 | tf_op jit(solution)/shard_map/ppermute | solution.py:383
  26.4 5.2 %collective-permute-start.2 = (f32[72,128]{1,0:T(8,128)S(1)}, f32[72,128]{1,0:T(8,128)S(1)}, u32[]{:S(2)}, u32[]{:S(2)}) collective-permute-start(f32[72,128]{1,0:T(8,128)S(1)} %reduce_sum.9), channel_id=1, source_target_pairs={{0,16},{8,24},{16,0},{24,8},{1,17},{9,25},{17,1},{25,9},{2,18},{10... | collective-permute-start | bytes 110600 | tf_op jit(solution)/shard_map/ppermute | solution.py:383
  27.1 4.6 %collective-permute-start.1 = (f32[72,128]{1,0:T(8,128)S(1)}, f32[72,128]{1,0:T(8,128)S(1)}, u32[]{:S(2)}, u32[]{:S(2)}) collective-permute-start(f32[72,128]{1,0:T(8,128)S(1)} %reduce_sum.9), channel_id=1, source_target_pairs={{0,8},{8,0},{16,24},{24,16},{1,9},{9,1},{17,25},{25,17},{2,10},{10... | collective-permute-start | bytes 110600 | tf_op jit(solution)/shard_map/ppermute | solution.py:383
  31.7 6.1 %collective-permute-start.6 = (f32[4,72,128]{2,1,0:T(8,128)S(1)}, f32[4,72,128]{2,1,0:T(8,128)S(1)}, u32[]{:S(2)}, u32[]{:S(2)}) collective-permute-start(f32[4,72,128]{2,1,0:T(8,128)S(1)} %pad_maximum_fusion.refs_0_), channel_id=1, source_target_pairs={{0,6},{2,4},{4,2},{6,0},{1,7},{3,5},{5,3},{7,1},{8,14},{10,12},{12... | collective-permute-start | bytes 442376 | tf_op jit(solution)/shard_map/ppermute | solution.py:376
  33.5 6.0 %collective-permute-start.5 = (f32[4,72,128]{2,1,0:T(8,128)S(1)}, f32[4,72,128]{2,1,0:T(8,128)S(1)}, u32[]{:S(2)}, u32[]{:S(2)}) collective-permute-start(f32[4,72,128]{2,1,0:T(8,128)S(1)} %pad_maximum_fusion.refs_0_), channel_id=1, source_target_pairs={{0,4},{4,0},{1,5},{5,1},{2,6},{6,2},{3,7},{7,3},{8,12},{12,8},{9,1... | collective-permute-start | bytes 442376 | tf_op jit(solution)/shard_map/ppermute | solution.py:376
  34.8 5.1 %collective-permute-start.4 = (f32[4,72,128]{2,1,0:T(8,128)S(1)}, f32[4,72,128]{2,1,0:T(8,128)S(1)}, u32[]{:S(2)}, u32[]{:S(2)}) collective-permute-start(f32[4,72,128]{2,1,0:T(8,128)S(1)} %pad_maximum_fusion.refs_0_), channel_id=1, source_target_pairs={{0,2},{2,0},{1,3},{3,1},{4,6},{6,4},{5,7},{7,5},{8,10},{10,8},{9,1... | collective-permute-start | bytes 442376 | tf_op jit(solution)/shard_map/ppermute | solution.py:376
  35.3 4.7 %collective-permute-start.7 = (f32[4,72,128]{2,1,0:T(8,128)S(1)}, f32[4,72,128]{2,1,0:T(8,128)S(1)}, u32[]{:S(2)}, u32[]{:S(2)}) collective-permute-start(f32[4,72,128]{2,1,0:T(8,128)S(1)} %pad_maximum_fusion.refs_0_), channel_id=1, source_target_pairs={{0,1},{1,0},{2,3},{3,2},{4,5},{5,4},{6,7},{7,6},{8,9},{9,8},{10,11... | collective-permute-start | bytes 442376 | tf_op jit(solution)/shard_map/ppermute | solution.py:376
  37.8 2.2 %collective-permute-start.10 = (f32[4,72,128]{2,1,0:T(8,128)S(1)}, f32[4,72,128]{2,1,0:T(8,128)S(1)}, u32[]{:S(2)}, u32[]{:S(2)}) collective-permute-start(f32[4,72,128]{2,1,0:T(8,128)S(1)} %collective-permute-done.6.refs_3_), channel_id=1, source_target_pairs={{0,1},{1,0},{2,3},{3,2},{4,5},{5,4},{6,7},{7,6},{8,9},{9,8},{10,11... | collective-permute-start | bytes 442376 | tf_op jit(solution)/shard_map/ppermute | solution.py:376
  39.5 1.4 %collective-permute-start.9 = (f32[4,72,128]{2,1,0:T(8,128)S(1)}, f32[4,72,128]{2,1,0:T(8,128)S(1)}, u32[]{:S(2)}, u32[]{:S(2)}) collective-permute-start(f32[4,72,128]{2,1,0:T(8,128)S(1)} %collective-permute-done.5.refs_2_), channel_id=1, source_target_pairs={{0,1},{1,0},{2,3},{3,2},{4,5},{5,4},{6,7},{7,6},{8,9},{9,8},{10,11... | collective-permute-start | bytes 442376 | tf_op jit(solution)/shard_map/ppermute | solution.py:376
  39.9 1.4 %collective-permute-start.8 = (f32[4,72,128]{2,1,0:T(8,128)S(1)}, f32[4,72,128]{2,1,0:T(8,128)S(1)}, u32[]{:S(2)}, u32[]{:S(2)}) collective-permute-start(f32[4,72,128]{2,1,0:T(8,128)S(1)} %collective-permute-done.4.refs_1_), channel_id=1, source_target_pairs={{0,1},{1,0},{2,3},{3,2},{4,5},{5,4},{6,7},{7,6},{8,9},{9,8},{10,11... | collective-permute-start | bytes 442376 | tf_op jit(solution)/shard_map/ppermute | solution.py:376

commit v5 on v4

--- a/solution.py
+++ b/solution.py
@@ -14,7 +14,7 @@
 SIDE = PICKED - B
 PACKED = 2 * SIDE + B + 8
 LOADS = 4
-AHEAD = 2
+AHEAD = 3
 F32 = jnp.float32
 BF16 = jnp.bfloat16
 VMEM_LIMIT = 48 * 2**20

time: 58.9 us -> 58.5 us (level)
  no operation moved by 1% of the time
where the time goes in v5:
time: 58.5 us; the launch traced here: 58.2 us
  Pallas kernels  19.8 us (34%)
  blocking collectives  15.9 us (27%)
  waiting for transfers between devices  10.7 us (18%)
  starting transfers between devices  9.49 us (16%)
  local copies, waits for them, and re-layouts  1.5 us (3%)
  between operations  0.84 us (1%)
    pallas_call x1, Pallas kernels, shards(): pl.pallas_call(solve_kernel, out_shape=[jax.ShapeDtypeStruct((width // fe...  16.8 us
    all_to_all x1, blocking collectives, shards(): lax.all_to_all(partial.reshape(tm_count, chunk, B), ('z', 'x'), 0, 0)  15.9 us
    ppermute x7, waiting for transfers between devices, swap(): return lax.ppermute(shard, axes, [(i, last - i) for i in range(last + 1)])  5.96 us
    ppermute x3, starting transfers between devices, gather_line(): lax.ppermute(piece, 'z', [(i, i ^ m) for i in range(count)])  4.45 us
    ppermute x7, starting transfers between devices, swap(): return lax.ppermute(shard, axes, [(i, last - i) for i in range(last + 1)])  3.63 us
    pallas_call x1, Pallas kernels, shards(): pl.pallas_call(gram_kernel, out_shape=[jax.ShapeDtypeStruct((2 * PICKED,...  2.72 us
    ppermute x1, waiting for transfers between devices, shards(): lax.ppermute(features[:LAG], ('z', 'x'), [(i, i - 1) for i in range(1, tm...  2.4 us
    ppermute x3, waiting for transfers between devices, gather_line(): lax.ppermute(piece, 'z', [(i, i ^ m) for i in range(count)])  2.33 us
  transfers between devices with their start and end apart: 11, of which 9 were waited for; matrix products, arithmetic and copies ran while one was open for 0% of the time, Pallas kernels for 5%

profile of v5, /device:TPU:0, one launch (start us, length us, event | category | flops | bytes accessed | tf_op | source)
XLA Modules:
  0.0 58.2 jit_solution(1758917686794121374)
XLA Ops:
  0.6 0.8 %slice.3 = bf16[64,512]{1,0:T(8,128)(2,1)S(1)} slice(bf16[2048,512]{1,0:T(8,128)(2,1)} %refs_8_.1), slice={[0:64], [0:512]} | slice | bytes 131072 | tf_op jit(solution)/shard_map/slice | solution.py:396
  1.5 0.0 copy-start
  1.5 1.4 %collective-permute-start = (bf16[64,512]{1,0:T(8,128)(2,1)S(1)}, bf16[64,512]{1,0:T(8,128)(2,1)S(1)}, u32[]{:S(2)}, u32[]{:S(2)}) collective-permute-start(bf16[64,512]{1,0:T(8,128)(2,1)S(1)} %slice.3), channel_id=1, source_target_pairs={{4,0},{8,4},{12,8},{16,12},{20,16},{24,20},{28,24},{5,1},{9,5},{13... | collective-permute-start | bytes 196616 | tf_op jit(solution)/shard_map/ppermute | solution.py:396
  2.9 0.0 copy-start.1
  2.9 0.6 %copy-done.1 = s32[16]{0:T(128)S(1)} copy-done((s32[16]{0:T(128)S(1)}, s32[16]{0:T(128)}, u32[]{:S(2)}) %copy-start.1) | copy-done | bytes 88
  3.6 0.0 copy-start.2
  3.6 2.7 %grams.1 = (f32[640,128]{1,0:T(8,128)S(1)}, bf16[64,512]{1,0:T(8,128)(2,1)S(1)}, f32[8,128]{1,0:T(8,128)S(1)}) custom-call(s32[16]{0:T(128)S(1)} %copy-done.1, bf16[2048,512]{1,0:T(8,128)(2,1)} %refs_8_.1), custom_call_target="tpu_custom_call" | custom-call | flops 603979776 | bytes 2097152 | tf_op jit(solution)/shard_map/grams/pallas_call | solution.py:402
  6.3 2.4 %collective-permute-done.halo_ref.refs_9_ = bf16[64,512]{1,0:T(8,128)(2,1)S(1)} collective-permute-done((bf16[64,512]{1,0:T(8,128)(2,1)S(1)}, bf16[64,512]{1,0:T(8,128)(2,1)S(1)}, u32[]{:S(2)}, u32[]{:S(2)}) %collective-permute-start) | collective-permute-done | bytes 65568 | tf_op jit(solution)/shard_map/ppermute | solution.py:396
  8.7 0.3 edges.1
  9.0 15.9 %all_to_all.5 = f32[8,72,128]{2,1,0:T(8,128)S(1)} all-to-all(f32[8,72,128]{2,1,0:T(8,128)S(1)} %bitcast.5), channel_id=1, replica_groups=mesh['z'=4,'x'=2,'y'=2,'c'=2] {'z','x'}, dimensions={0} | all-to-all | bytes 589824 | tf_op jit(solution)/shard_map/all_to_all | solution.py:431
  24.9 1.5 %collective-permute-start.3 = (f32[72,128]{1,0:T(8,128)S(1)}, f32[72,128]{1,0:T(8,128)S(1)}, u32[]{:S(2)}, u32[]{:S(2)}) collective-permute-start(f32[72,128]{1,0:T(8,128)S(1)} %reduce_sum.9), channel_id=1, source_target_pairs={{0,24},{8,16},{16,8},{24,0},{1,25},{9,17},{17,9},{25,1},{2,26},{10... | collective-permute-start | bytes 110600 | tf_op jit(solution)/shard_map/ppermute | solution.py:383
  26.4 0.7 %collective-permute-start.2 = (f32[72,128]{1,0:T(8,128)S(1)}, f32[72,128]{1,0:T(8,128)S(1)}, u32[]{:S(2)}, u32[]{:S(2)}) collective-permute-start(f32[72,128]{1,0:T(8,128)S(1)} %reduce_sum.9), channel_id=1, source_target_pairs={{0,16},{8,24},{16,0},{24,8},{1,17},{9,25},{17,1},{25,9},{2,18},{10... | collective-permute-start | bytes 110600 | tf_op jit(solution)/shard_map/ppermute | solution.py:383
  27.1 2.3 %collective-permute-start.1 = (f32[72,128]{1,0:T(8,128)S(1)}, f32[72,128]{1,0:T(8,128)S(1)}, u32[]{:S(2)}, u32[]{:S(2)}) collective-permute-start(f32[72,128]{1,0:T(8,128)S(1)} %reduce_sum.9), channel_id=1, source_target_pairs={{0,8},{8,0},{16,24},{24,16},{1,9},{9,1},{17,25},{25,17},{2,10},{10... | collective-permute-start | bytes 110600 | tf_op jit(solution)/shard_map/ppermute | solution.py:383
  29.4 1.4 %collective-permute-done.3 = f32[72,128]{1,0:T(8,128)S(1)} collective-permute-done((f32[72,128]{1,0:T(8,128)S(1)}, f32[72,128]{1,0:T(8,128)S(1)}, u32[]{:S(2)}, u32[]{:S(2)}) %collective-permute-start.3) | collective-permute-done | bytes 36896 | tf_op jit(solution)/shard_map/ppermute | solution.py:383
  30.7 0.9 %collective-permute-done.2 = f32[72,128]{1,0:T(8,128)S(1)} collective-permute-done((f32[72,128]{1,0:T(8,128)S(1)}, f32[72,128]{1,0:T(8,128)S(1)}, u32[]{:S(2)}, u32[]{:S(2)}) %collective-permute-start.2) | collective-permute-done | bytes 36896 | tf_op jit(solution)/shard_map/ppermute | solution.py:383
  31.6 0.1 collective-permute-done.1
  31.7 1.8 %collective-permute-start.6 = (f32[4,72,128]{2,1,0:T(8,128)S(1)}, f32[4,72,128]{2,1,0:T(8,128)S(1)}, u32[]{:S(2)}, u32[]{:S(2)}) collective-permute-start(f32[4,72,128]{2,1,0:T(8,128)S(1)} %pad_maximum_fusion.refs_0_), channel_id=1, source_target_pairs={{0,6},{2,4},{4,2},{6,0},{1,7},{3,5},{5,3},{7,1},{8,14},{10,12},{12... | collective-permute-start | bytes 442376 | tf_op jit(solution)/shard_map/ppermute | solution.py:376
  33.5 1.3 %collective-permute-start.5 = (f32[4,72,128]{2,1,0:T(8,128)S(1)}, f32[4,72,128]{2,1,0:T(8,128)S(1)}, u32[]{:S(2)}, u32[]{:S(2)}) collective-permute-start(f32[4,72,128]{2,1,0:T(8,128)S(1)} %pad_maximum_fusion.refs_0_), channel_id=1, source_target_pairs={{0,4},{4,0},{1,5},{5,1},{2,6},{6,2},{3,7},{7,3},{8,12},{12,8},{9,1... | collective-permute-start | bytes 442376 | tf_op jit(solution)/shard_map/ppermute | solution.py:376
  34.8 0.5 collective-permute-start.4
  35.3 0.0 collective-permute-start.7
  35.3 2.5 %collective-permute-done.6.refs_3_ = f32[4,72,128]{2,1,0:T(8,128)S(1)} collective-permute-done((f32[4,72,128]{2,1,0:T(8,128)S(1)}, f32[4,72,128]{2,1,0:T(8,128)S(1)}, u32[]{:S(2)}, u32[]{:S(2)}) %collective-permute-start.6) | collective-permute-done | bytes 147488 | tf_op jit(solution)/shard_map/ppermute | solution.py:376
  37.8 0.0 collective-permute-start.10
  37.8 1.7 %collective-permute-done.5.refs_2_ = f32[4,72,128]{2,1,0:T(8,128)S(1)} collective-permute-done((f32[4,72,128]{2,1,0:T(8,128)S(1)}, f32[4,72,128]{2,1,0:T(8,128)S(1)}, u32[]{:S(2)}, u32[]{:S(2)}) %collective-permute-start.5) | collective-permute-done | bytes 147488 | tf_op jit(solution)/shard_map/ppermute | solution.py:376
  39.5 0.0 collective-permute-start.9
  39.5 0.4 collective-permute-done.4.refs_1_
  39.9 0.1 collective-permute-start.8
  40.0 0.0 collective-permute-done.7.refs_4_
  40.0 0.0 collective-permute-done.10.refs_7_
  40.0 0.9 %collective-permute-done.9.refs_6_ = f32[4,72,128]{2,1,0:T(8,128)S(1)} collective-permute-done((f32[4,72,128]{2,1,0:T(8,128)S(1)}, f32[4,72,128]{2,1,0:T(8,128)S(1)}, u32[]{:S(2)}, u32[]{:S(2)}) %collective-permute-start.9) | collective-permute-done | bytes 147488 | tf_op jit(solution)/shard_map/ppermute | solution.py:376
  40.9 0.4 collective-permute-done.8.refs_5_
  41.3 0.0 copy-done
  41.3 0.0 copy-done.2
  41.3 16.8 %solve.1 = (f32[128,512]{1,0:T(8,128)}, f32[32,2048]{1,0:T(8,128)}) custom-call(s32[16]{0:T(128)S(1)} %copy-done.2, f32[4,72,128]{2,1,0:T(8,128)S(1)} %pad_maximum_fusion.refs_0_, f32[4,72,128]{2,1,0:T(8,128)S(1)} %collective-permute-done.4.refs_1_, f32[4,72,128]{2,1,0:T(8,128)S(1)} %collective-permute-done.5.refs_2_, ...), custom_call_target="tpu_custom_call" | custom-call | tf_op jit(solution)/shard_map/solve/pallas_call | solution.py:436
  (2 shorter events, 0.0 us)
Async XLA Ops:
  1.5 39.8 %copy-start = (bf16[2048,512]{1,0:T(8,128)(2,1)S(1)}, bf16[2048,512]{1,0:T(8,128)(2,1)}, u32[]{:S(2)}) copy-start(bf16[2048,512]{1,0:T(8,128)(2,1)} %refs_8_.1) | copy-start | bytes 6291460
  1.5 7.2 %collective-permute-start = (bf16[64,512]{1,0:T(8,128)(2,1)S(1)}, bf16[64,512]{1,0:T(8,128)(2,1)S(1)}, u32[]{:S(2)}, u32[]{:S(2)}) collective-permute-start(bf16[64,512]{1,0:T(8,128)(2,1)S(1)} %slice.3), channel_id=1, source_target_pairs={{4,0},{8,4},{12,8},{16,12},{20,16},{24,20},{28,24},{5,1},{9,5},{13... | collective-permute-start | bytes 196616 | tf_op jit(solution)/shard_map/ppermute | solution.py:396
  2.9 0.7 %copy-start.1 = (s32[16]{0:T(128)S(1)}, s32[16]{0:T(128)}, u32[]{:S(2)}) copy-start(s32[16]{0:T(128)} %seg_ref.1) | copy-start | bytes 196
  3.6 37.8 %copy-start.2 = (s32[16]{0:T(128)S(1)}, s32[16]{0:T(128)}, u32[]{:S(2)}) copy-start(s32[16]{0:T(128)} %seg_ref.1) | copy-start | bytes 196
  24.9 5.8 %collective-permute-start.3 = (f32[72,128]{1,0:T(8,128)S(1)}, f32[72,128]{1,0:T(8,128)S(1)}, u32[]{:S(2)}, u32[]{:S(2)}) collective-permute-start(f32[72,128]{1,0:T(8,128)S(1)} %reduce_sum.9), channel_id=1, source_target_pairs={{0,24},{8,16},{16,8},{24,0},{1,25},{9,17},{17,9},{25,1},{2,26},{10... | collective-permute-start | bytes 110600 | tf_op jit(solution)/shard_map/ppermute | solution.py:383
  26.4 5.2 %collective-permute-start.2 = (f32[72,128]{1,0:T(8,128)S(1)}, f32[72,128]{1,0:T(8,128)S(1)}, u32[]{:S(2)}, u32[]{:S(2)}) collective-permute-start(f32[72,128]{1,0:T(8,128)S(1)} %reduce_sum.9), channel_id=1, source_target_pairs={{0,16},{8,24},{16,0},{24,8},{1,17},{9,25},{17,1},{25,9},{2,18},{10... | collective-permute-start | bytes 110600 | tf_op jit(solution)/shard_map/ppermute | solution.py:383
  27.1 4.6 %collective-permute-start.1 = (f32[72,128]{1,0:T(8,128)S(1)}, f32[72,128]{1,0:T(8,128)S(1)}, u32[]{:S(2)}, u32[]{:S(2)}) collective-permute-start(f32[72,128]{1,0:T(8,128)S(1)} %reduce_sum.9), channel_id=1, source_target_pairs={{0,8},{8,0},{16,24},{24,16},{1,9},{9,1},{17,25},{25,17},{2,10},{10... | collective-permute-start | bytes 110600 | tf_op jit(solution)/shard_map/ppermute | solution.py:383
  31.7 6.1 %collective-permute-start.6 = (f32[4,72,128]{2,1,0:T(8,128)S(1)}, f32[4,72,128]{2,1,0:T(8,128)S(1)}, u32[]{:S(2)}, u32[]{:S(2)}) collective-permute-start(f32[4,72,128]{2,1,0:T(8,128)S(1)} %pad_maximum_fusion.refs_0_), channel_id=1, source_target_pairs={{0,6},{2,4},{4,2},{6,0},{1,7},{3,5},{5,3},{7,1},{8,14},{10,12},{12... | collective-permute-start | bytes 442376 | tf_op jit(solution)/shard_map/ppermute | solution.py:376
  33.5 6.0 %collective-permute-start.5 = (f32[4,72,128]{2,1,0:T(8,128)S(1)}, f32[4,72,128]{2,1,0:T(8,128)S(1)}, u32[]{:S(2)}, u32[]{:S(2)}) collective-permute-start(f32[4,72,128]{2,1,0:T(8,128)S(1)} %pad_maximum_fusion.refs_0_), channel_id=1, source_target_pairs={{0,4},{4,0},{1,5},{5,1},{2,6},{6,2},{3,7},{7,3},{8,12},{12,8},{9,1... | collective-permute-start | bytes 442376 | tf_op jit(solution)/shard_map/ppermute | solution.py:376
  34.8 5.1 %collective-permute-start.4 = (f32[4,72,128]{2,1,0:T(8,128)S(1)}, f32[4,72,128]{2,1,0:T(8,128)S(1)}, u32[]{:S(2)}, u32[]{:S(2)}) collective-permute-start(f32[4,72,128]{2,1,0:T(8,128)S(1)} %pad_maximum_fusion.refs_0_), channel_id=1, source_target_pairs={{0,2},{2,0},{1,3},{3,1},{4,6},{6,4},{5,7},{7,5},{8,10},{10,8},{9,1... | collective-permute-start | bytes 442376 | tf_op jit(solution)/shard_map/ppermute | solution.py:376
  35.3 4.7 %collective-permute-start.7 = (f32[4,72,128]{2,1,0:T(8,128)S(1)}, f32[4,72,128]{2,1,0:T(8,128)S(1)}, u32[]{:S(2)}, u32[]{:S(2)}) collective-permute-start(f32[4,72,128]{2,1,0:T(8,128)S(1)} %pad_maximum_fusion.refs_0_), channel_id=1, source_target_pairs={{0,1},{1,0},{2,3},{3,2},{4,5},{5,4},{6,7},{7,6},{8,9},{9,8},{10,11... | collective-permute-start | bytes 442376 | tf_op jit(solution)/shard_map/ppermute | solution.py:376
  37.8 2.2 %collective-permute-start.10 = (f32[4,72,128]{2,1,0:T(8,128)S(1)}, f32[4,72,128]{2,1,0:T(8,128)S(1)}, u32[]{:S(2)}, u32[]{:S(2)}) collective-permute-start(f32[4,72,128]{2,1,0:T(8,128)S(1)} %collective-permute-done.6.refs_3_), channel_id=1, source_target_pairs={{0,1},{1,0},{2,3},{3,2},{4,5},{5,4},{6,7},{7,6},{8,9},{9,8},{10,11... | collective-permute-start | bytes 442376 | tf_op jit(solution)/shard_map/ppermute | solution.py:376
  39.5 1.4 %collective-permute-start.9 = (f32[4,72,128]{2,1,0:T(8,128)S(1)}, f32[4,72,128]{2,1,0:T(8,128)S(1)}, u32[]{:S(2)}, u32[]{:S(2)}) collective-permute-start(f32[4,72,128]{2,1,0:T(8,128)S(1)} %collective-permute-done.5.refs_2_), channel_id=1, source_target_pairs={{0,1},{1,0},{2,3},{3,2},{4,5},{5,4},{6,7},{7,6},{8,9},{9,8},{10,11... | collective-permute-start | bytes 442376 | tf_op jit(solution)/shard_map/ppermute | solution.py:376
  39.9 1.4 %collective-permute-start.8 = (f32[4,72,128]{2,1,0:T(8,128)S(1)}, f32[4,72,128]{2,1,0:T(8,128)S(1)}, u32[]{:S(2)}, u32[]{:S(2)}) collective-permute-start(f32[4,72,128]{2,1,0:T(8,128)S(1)} %collective-permute-done.4.refs_1_), channel_id=1, source_target_pairs={{0,1},{1,0},{2,3},{3,2},{4,5},{5,4},{6,7},{7,6},{8,9},{9,8},{10,11... | collective-permute-start | bytes 442376 | tf_op jit(solution)/shard_map/ppermute | solution.py:376
